TPU v7x, 256 devices: a whole 4x4x8 slice. The times are simulated.
256 devices in a mesh: dp: 16 (over x, y), tensor: 16 (over z, core).
Axes of the slice: x: 4, y: 4, z: 8, core: 2. Of those that a mesh axis runs over, the one named last changes fastest.
Arguments:
- context: bfloat16 [32, 1024, 4096], P('dp', None, 'tensor'), may hold values from -6 to 6
- out_grad: bfloat16 [32, 1024, 4608], P('dp', None, 'tensor'), may hold values from -40 to 40
- example_user: int32 [32], replicated, may hold values from 0 to 15, as said below
- user_counts: int32 [16], replicated, may hold values from 1 to 4, as said below
Outputs:
- weight_grad: float32 [4096, 4608], P('dp', 'tensor')
Inputs may be any that keep to these rules, and one draw needn't show every extreme that they name: `example_user`: every user id occurs; user u occurs exactly user_counts[u] times. user_counts[u] counts the examples of user u; they sum to 32.
All inputs are finite; a program needn't handle non-finite values.
Results may differ from a plain program's by a relative error of at most 0.0008.
Values may be sent and summed in bfloat16 or wider, within the bound.
A program may use at most 128 MiB of HBM per device.

v0:
```python
import math

import jax
import jax.numpy as jnp
from jax import lax
from jax.sharding import PartitionSpec as P


def per_device(context, out_grad, example_user, user_counts):
    local_count = context.shape[0]
    seq_len = context.shape[1]
    user_total = user_counts.shape[0]
    tensor_size = lax.axis_size("tensor")
    width_in = context.shape[2] * tensor_size
    width_out = out_grad.shape[2] * tensor_size
    data_index = lax.axis_index("dp")
    own_users = lax.dynamic_slice_in_dim(example_user, data_index * local_count, local_count)
    user_range = jnp.arange(user_total, dtype=jnp.int32)
    own_onehot = (own_users[:, None] == user_range[None, :]).astype(jnp.float32)
    gathered = lax.all_gather(context, "tensor", axis=2, tiled=True)
    row_share = seq_len // tensor_size
    own_rows = lax.dynamic_slice_in_dim(
        gathered, lax.axis_index("tensor") * row_share, row_share, 1
    )
    context_part = jnp.einsum(
        "etk,esk->ets", own_rows, gathered, preferred_element_type=jnp.float32
    )
    grad_gram = jnp.einsum("etk,esk->ets", out_grad, out_grad, preferred_element_type=jnp.float32)
    grad_part = lax.psum_scatter(
        grad_gram.astype(jnp.bfloat16), "tensor", scatter_dimension=1, tiled=True
    ).astype(jnp.float32)
    partial_square = jnp.sum(context_part * grad_part, axis=(1, 2))
    full_square = lax.psum(partial_square, "tensor")
    example_norm = jnp.sqrt(full_square + 1e-06)
    user_local = jnp.sum(example_norm[:, None] * own_onehot, axis=0)
    user_norm = lax.psum(user_local, "dp")
    counts_float = user_counts.astype(jnp.float32)
    clip_bound = 1.5 * math.sqrt(width_in * width_out)
    user_weight = jnp.minimum(1.0, clip_bound * counts_float / user_norm) / (
        counts_float * user_total
    )
    example_weight = jnp.sum(own_onehot * user_weight[None, :], axis=1)
    block_terms = jnp.einsum("etk,etn->ekn", gathered, out_grad, preferred_element_type=jnp.float32)
    return lax.psum_scatter(
        jnp.sum(example_weight[:, None, None] * block_terms, axis=0),
        "dp",
        scatter_dimension=0,
        tiled=True,
    )


def solution(mesh):
    in_specs = (P("dp", None, "tensor"), P("dp", None, "tensor"), P(), P())
    out_specs = P("dp", "tensor")
    return jax.shard_map(
        per_device, mesh=mesh, in_specs=in_specs, out_specs=out_specs, check_vma=False
    )
```

profile of v0, /device:TPU:1, one launch (start us, length us, event | category | flops | bytes accessed | tf_op | source)
XLA Modules:
  0.0 355.3 jit_solution(17204341248907605595)
XLA Ops:
  6.5 0.0 copy-start
  6.5 0.0 reduce-scatter.3.cloned.1.call-start
  6.5 1.3 copy-done
  7.8 4.3 %convolution_convert_fusion = bf16[2,1024,1024]{2,1,0:T(8,128)(2,1)} fusion(bf16[2,1024,288]{1,2,0:T(8,128)(2,1)S(1)} %copy-done), kind=kOutput, calls=%fused_computation.1 | convolution fusion | flops 1210056704 | bytes 5373952 | tf_op jit(solution)/shard_map/etk,esk->ets/dot_general | solution.py:28
  12.1 0.0 reduce-scatter.3.cloned.1.call-update
  12.1 0.0 all-gather.2.cloned.1.call-start
  12.2 0.7 all-gather.2.cloned.1.call-update
  12.9 0.0 reduce-scatter.5.cloned.1.call-start
  12.9 0.0 copy-start.1
  13.0 0.0 copy-start.2
  13.0 62.8 %reduce-scatter.3.cloned.1.call-done = bf16[2,64,1024]{2,1,0:T(8,128)(2,1)} async-done(((bf16[2,1024,1024]{2,1,0:T(8,128)(2,1)}), bf16[2,64,1024]{2,1,0:T(8,128)(2,1)}) %reduce-scatter.3.cloned.1.call-update) | async-done | bytes 262160 | tf_op jit(solution)/shard_map/reduce_scatter | solution.py:29
  75.7 106.7 %all-gather.2.cloned.1.call-done = bf16[2,1024,4096]{2,1,0:T(8,128)(2,1)} async-done(((bf16[2,1024,256]{2,1,0:T(8,128)(2,1)}), bf16[2,1024,4096]{2,1,0:T(8,128)(2,1)}) %all-gather.2.cloned.1.call-update) | async-done | bytes 16777232 | tf_op jit(solution)/shard_map/all_gather | solution.py:20
  182.5 11.4 %fusion = f32[2]{0:T(128)S(1)} fusion(bf16[2,1024,4096]{2,1,0:T(8,128)(2,1)} %all-gather.2.cloned.1.call-done, s32[]{:T(128)S(6)} %select_n.7, bf16[2,64,1024]{2,1,0:T(8,128)(2,1)} %reduce-scatter.3.cloned.1.call-done), kind=kOutput, calls=%fused_computation.3 | convolution fusion | flops 1074135040 | bytes 18087948 | tf_op jit(solution)/shard_map/etk,esk->ets/dot_general | solution.py:25
  193.9 0.0 copy-done.1
  193.9 0.1 dynamic_slice.6
  193.9 23.1 %psum.14 = f32[2]{0:T(128)S(1)} all-reduce(f32[2]{0:T(128)S(1)} %fusion), channel_id=1, replica_groups=mesh['dp'=16,'tensor'=16] {'tensor'}, use_global_device_ids=true, to_apply=%region_2.0 | all-reduce | flops 2 | bytes 16 | tf_op jit(solution)/shard_map/psum | solution.py:33
  217.1 0.1 select_reduce_fusion.1
  217.2 33.1 %psum.15 = f32[16]{0:T(128)S(1)} all-reduce(f32[16]{0:T(128)S(1)} %select_reduce_fusion.1), channel_id=1, replica_groups=mesh['dp'=16,'tensor'=16] {'dp'}, use_global_device_ids=true, to_apply=%region_4.0 | all-reduce | flops 16 | bytes 128 | tf_op jit(solution)/shard_map/psum | solution.py:36
  250.2 0.0 copy-done.2
  250.2 0.2 select_reduce_fusion
  250.4 14.0 %multiply_reduce_fusion = f32[4096,288]{0,1:T(8,128)} fusion(bf16[2,1024,288]{1,2,0:T(8,128)(2,1)S(1)} %copy-done, bf16[2,1024,4096]{2,1,0:T(8,128)(2,1)} %all-gather.2.cloned.1.call-done, f32[2]{0:T(128)S(1)} %select_reduce_fusion), kind=kOutput, calls=%fused_computation | convolution fusion | flops 4835377152 | bytes 22675464 | tf_op jit(solution)/shard_map/etk,etn->ekn/dot_general | solution.py:43
  264.4 0.0 reduce-scatter.5.cloned.1.call-update
  264.4 84.3 %reduce-scatter.5.cloned.1.call-done = f32[256,288]{0,1:T(8,128)} async-done(((f32[4096,288]{0,1:T(8,128)}), f32[256,288]{0,1:T(8,128)}) %reduce-scatter.5.cloned.1.call-update) | async-done | bytes 294928 | tf_op jit(solution)/shard_map/reduce_scatter | solution.py:44
  (2 shorter events, 0.0 us)
Async XLA Ops:
  6.5 1.3 copy-start
  6.5 69.2 %reduce-scatter.3.cloned.1.call-start = ((), (), s32[]{:S(2)}) async-start(), calls=%async_computation.3 | async-start | bytes 4456448 | tf_op jit(solution)/shard_map/reduce_scatter | solution.py:29
  12.1 170.3 %all-gather.2.cloned.1.call-start = ((), (), s32[]{:S(2)}) async-start(), calls=%async_computation.2 | async-start | bytes 17825792 | tf_op jit(solution)/shard_map/all_gather | solution.py:20
  12.9 335.9 %reduce-scatter.5.cloned.1.call-start = ((), (), s32[]{:S(2)}) async-start(), calls=%async_computation.4 | async-start | bytes 5013504 | tf_op jit(solution)/shard_map/reduce_scatter | solution.py:44
  12.9 180.9 %copy-start.1 = (s32[32]{0:T(128)S(1)}, s32[32]{0:T(128)}, u32[]{:S(2)}) copy-start(s32[32]{0:T(128)} %param.6) | copy-start | bytes 388
  13.0 237.3 %copy-start.2 = (s32[16]{0:T(128)S(1)}, s32[16]{0:T(128)}, u32[]{:S(2)}) copy-start(s32[16]{0:T(128)} %param.7) | copy-start | bytes 196
Sparse Core Ops, SparseCore 0:
  12.3 63.4 reduce-scatter.2
  77.5 104.9 all-gather.1
  264.6 84.1 reduce-scatter.4
where the time goes:
time: 356 us; the launch traced here: 355 us
  waiting for transfers between devices  255 us (72%)
  blocking collectives  56.2 us (16%)
  matrix products  29.7 us (8%)
  between operations  13.1 us (4%)
    all_gather x1, waiting for transfers between devices, per_device(): gathered = lax.all_gather(context, 'tensor', axis=2, tiled=True)  107 us
    reduce_scatter x1, waiting for transfers between devices, per_device(): lax.psum_scatter(jnp.sum(example_weight[:, None, None] * block_terms, axi...  84.3 us
    reduce_scatter x1, waiting for transfers between devices, per_device(): lax.psum_scatter(grad_gram.astype(jnp.bfloat16), 'tensor', scatter_dimens...  62.8 us
    psum x1, blocking collectives, per_device(): user_norm = lax.psum(user_local, 'dp')  33.1 us
    psum x1, blocking collectives, per_device(): full_square = lax.psum(partial_square, 'tensor')  23.1 us
    dot_general x1, matrix products, per_device(): jnp.einsum('etk,etn->ekn', gathered, out_grad, preferred_element_type=jnp...  14 us
    dot_general x1, matrix products, per_device(): jnp.einsum('etk,esk->ets', own_rows, gathered, preferred_element_type=jnp...  11.4 us
  transfers between devices with their start and end apart: 3, of which 3 were waited for; matrix products, arithmetic and copies ran while one was open for 0% of the time, Pallas kernels for 0%

commit v1 on v0

v1 whole, which is shorter than its diff:
```python
import functools
import math

import jax
import jax.numpy as jnp
from jax import lax
from jax.experimental import pallas as pl
from jax.experimental.pallas import tpu as pltpu
from jax.sharding import PartitionSpec as P

MESH = pl.DeviceIdType.MESH
F32 = jnp.float32
SIDE = 4
RING = 8
GROUP = 16
STAGES = RING - 1


def kernel(clip_bound, context, grad, users, counts, out, held, grad_in, grad_t, terms, mask,
           squares, square_box, norm_box, first_box, group_box, second_box, last_box,
           local_sem, ring_send, ring_recv, side_send, square_send, square_recv,
           norm_send, norm_recv, sum_send, sum_recv):
    data, tensor = lax.axis_index("dp"), lax.axis_index("tensor")
    depth, core = lax.div(tensor, 2), lax.rem(tensor, 2)
    place = (lax.div(data, SIDE), lax.rem(data, SIDE))
    half = terms.shape[3] // 2

    def on_ring(step):
        return lax.rem(depth + step + RING, RING)

    right = (data, on_ring(1) * 2 + core)
    left = (data, on_ring(-1) * 2 + core)
    sibling = (data, depth * 2 + 1 - core)

    load_grad = pltpu.make_async_copy(grad, grad_in, local_sem.at[0])
    load_grad.start()
    load_own = pltpu.make_async_copy(context, held.at[tensor], local_sem.at[1])
    load_own.start()

    barrier = pltpu.get_barrier_semaphore()

    @pl.loop(1, GROUP)
    def _(step):
        pl.semaphore_signal(barrier, inc=1, device_id=(data, lax.rem(tensor + step, GROUP)), device_id_type=MESH)
        pl.semaphore_signal(barrier, inc=1, device_id=(lax.rem(data + step, GROUP), tensor), device_id_type=MESH)

    pl.semaphore_wait(barrier, 2 * (GROUP - 1))

    def chunk_copy(src, slot, example, send_sem, device):
        return pltpu.make_async_remote_copy(
            src_ref=src, dst_ref=held.at[slot, example], send_sem=send_sem,
            recv_sem=ring_recv.at[slot, example], device_id=device, device_id_type=MESH)

    for turn in range(2):
        chunk_copy(context.at[turn], tensor, turn, ring_send.at[0, turn], right).start()
        chunk_copy(context.at[1 - turn], tensor, 1 - turn, ring_send.at[1, turn], left).start()
    for turn in range(2):
        chunk_copy(context.at[turn], tensor, turn, side_send.at[0, turn], sibling).start()

    squares[...] = jnp.zeros_like(squares)
    load_grad.wait()
    for example in range(2):
        grad_t[example] = grad_in[example].T

    @pl.loop(0, 2 * GROUP)
    def _(item):
        for example in range(2):
            same = jnp.where(users[item] == users[2 * data + example], 1.0, 0.0)
            mask[example, item] = jnp.full(mask.shape[2:], same, F32)

    def product(slot, example):
        term = jnp.dot(grad_t[example], held[slot, example], preferred_element_type=F32)
        term = term.reshape(terms.shape[3:])
        terms[example, lax.div(slot, SIDE), lax.rem(slot, SIDE)] = term
        squares[example] += jnp.sum(term * term, axis=0)

    def arrived(slot, example):
        chunk_copy(context.at[0], slot, example, ring_send.at[0, 0], right).wait_recv()

    load_own.wait()
    for example in range(2):
        product(tensor, example)
    for example in range(2):
        arrived(depth * 2 + 1 - core, example)
        product(depth * 2 + 1 - core, example)

    @pl.loop(0, STAGES)
    def _(stage):
        distance = 1 + lax.div(stage, 2)
        turn = lax.rem(stage, 2)
        sources = ((on_ring(-distance), turn), (on_ring(distance), 1 - turn))
        for way, (source, example) in enumerate(sources):
            slot = source * 2 + core
            arrived(slot, example)

            @pl.when(stage < STAGES - 2)
            def _():
                chunk_copy(held.at[slot, example], slot, example, ring_send.at[way, 2 + stage],
                           (right, left)[way]).start()

            chunk_copy(held.at[slot, example], slot, example, side_send.at[way, 2 + stage], sibling).start()
        for source, example in sources:
            product(source * 2 + core, example)
        for source, example in sources:
            arrived(source * 2 + 1 - core, example)
            product(source * 2 + 1 - core, example)

    folded = squares[:, :, :128] + squares[:, :, 128:]
    square_box[tensor] = folded

    def square_copy(step):
        return pltpu.make_async_remote_copy(
            src_ref=square_box.at[tensor], dst_ref=square_box.at[tensor], send_sem=square_send.at[step],
            recv_sem=square_recv.at[tensor], device_id=(data, lax.rem(tensor + step, GROUP)), device_id_type=MESH)

    def square_arrival(step):
        peer = lax.rem(tensor + step, GROUP)
        return pltpu.make_async_remote_copy(
            src_ref=square_box.at[peer], dst_ref=square_box.at[peer], send_sem=square_send.at[step],
            recv_sem=square_recv.at[peer], device_id=(data, peer), device_id_type=MESH)

    @pl.loop(1, GROUP)
    def _(step):
        square_copy(step).start()

    @pl.loop(1, GROUP)
    def _(step):
        square_arrival(step).wait_recv()

    total = jnp.sum(square_box[...], axis=0)
    total = jnp.sum(jnp.sum(total, axis=2, keepdims=True), axis=1, keepdims=True)
    norm_box[data] = jnp.broadcast_to(jnp.sqrt(total + 1e-6), norm_box.shape[1:])

    def norm_copy(step):
        return pltpu.make_async_remote_copy(
            src_ref=norm_box.at[data], dst_ref=norm_box.at[data], send_sem=norm_send.at[step],
            recv_sem=norm_recv.at[data], device_id=(lax.rem(data + step, GROUP), tensor), device_id_type=MESH)

    def norm_arrival(step):
        peer = lax.rem(data + step, GROUP)
        return pltpu.make_async_remote_copy(
            src_ref=norm_box.at[peer], dst_ref=norm_box.at[peer], send_sem=norm_send.at[step],
            recv_sem=norm_recv.at[peer], device_id=(peer, tensor), device_id_type=MESH)

    @pl.loop(1, GROUP)
    def _(step):
        norm_copy(step).start()

    @pl.loop(1, GROUP)
    def _(step):
        norm_arrival(step).wait_recv()

    norms = norm_box[...].reshape((2 * GROUP,) + norm_box.shape[2:])
    weights = []
    for example in range(2):
        user_norm = jnp.sum(norms * mask[example], axis=0)
        count = counts[users[2 * data + example]].astype(F32)
        weight = jnp.minimum(1.0, clip_bound * count / user_norm) / (count * counts.shape[0])
        weights.append(jnp.concatenate([weight, weight], axis=1))

    def neighbour(dim, step):
        moved = list(place)
        moved[dim] = lax.rem(place[dim] + step + SIDE, SIDE)
        return (moved[0] * SIDE + moved[1], tensor)

    def along(dim, step):
        return lax.rem(place[dim] + step + SIDE, SIDE)

    def weighed(index):
        return weights[0] * terms[(0,) + index] + weights[1] * terms[(1,) + index]

    def spot(part, main, other, span):
        return (main, other, span) if part == 0 else (other, main, span)

    def sum_copy(part, phase, message, way, src, dst):
        number = ((part * 2 + phase) * 3 + message) * 2 + way
        dim = part if phase == 0 else 1 - part
        return pltpu.make_async_remote_copy(
            src_ref=src, dst_ref=dst, send_sem=sum_send.at[number], recv_sem=sum_recv.at[number],
            device_id=neighbour(dim, 1 if way == 0 else -1), device_id_type=MESH)

    pairs = (pl.ds(0, 2), pl.ds(2, 2))
    copies = []
    merges = []
    spans = (pl.ds(0, half), pl.ds(half, half))

    def send(*args):
        copy = sum_copy(*args)
        copy.start()
        copies.append(copy)
        return copy

    firsts, raws, joined = {}, {}, {}
    for part in range(2):
        for way in range(2):
            index = spot(part, along(part, 2), pairs[way], spans[part])
            terms[(0,) + index] = weighed(index)
            firsts[part, way] = send(part, 0, 0, way, terms.at[(0,) + index], first_box.at[part, way])
    for part in range(2):
        for way in range(2):
            index = spot(part, along(part, 1 if way == 0 else -1), pairs[1 - way], spans[part])
            terms[(0,) + index] = weighed(index)
            raws[part, way] = send(part, 0, 1, way, terms.at[(0,) + index], group_box.at[part, way, pairs[1 - way]])
    for part in range(2):
        for way in range(2):
            index = spot(part, along(part, 1 if way == 0 else -1), pairs[way], spans[part])
            firsts[part, way].wait_recv()
            terms[(0,) + index] = weighed(index) + first_box[part, way]
            joined[part, way] = send(part, 0, 2, way, terms.at[(0,) + index], group_box.at[part, way, pairs[way]])
    for part in range(2):
        for way in range(2):
            index = spot(part, place[part], pairs[way], spans[part])
            terms[(0,) + index] = weighed(index)
    for part in range(2):
        for way in range(2):
            raws[part, way].wait_recv()
            joined[part, way].wait_recv()
        index = spot(part, place[part], pl.ds(0, SIDE), spans[part])
        terms[(0,) + index] = terms[(0,) + index] + (group_box[part, 0] + group_box[part, 1])

    quarter = half // 2
    lows = (pl.ds(0, quarter), pl.ds(quarter, quarter))

    def piece(part, step, way):
        start = part * half + way * quarter
        return spot(part, place[part], along(1 - part, step), pl.ds(start, quarter))

    for part in range(2):
        for way in range(2):
            index = piece(part, 2, way)
            firsts[part, way] = send(part, 1, 0, way, terms.at[(0,) + index], second_box.at[part, way])
    for part in range(2):
        for way in range(2):
            index = piece(part, 1 if way == 0 else -1, 1 - way)
            raws[part, way] = send(part, 1, 1, way, terms.at[(0,) + index], last_box.at[part, way, lows[1 - way]])
    for part in range(2):
        for way in range(2):
            index = piece(part, 1 if way == 0 else -1, way)
            firsts[part, way].wait_recv()
            terms[(0,) + index] = terms[(0,) + index] + second_box[part, way]
            joined[part, way] = send(part, 1, 2, way, terms.at[(0,) + index], last_box.at[part, way, lows[way]])
    for part in range(2):
        for way in range(2):
            raws[part, way].wait_recv()
            joined[part, way].wait_recv()
        own = spot(part, place[part], place[1 - part], spans[part])
        out[spans[part]] = terms[(0,) + own] + (last_box[part, 0] + last_box[part, 1])

    for copy in copies:
        copy.wait_send()

    @pl.loop(1, GROUP)
    def _(step):
        square_copy(step).wait_send()
        norm_copy(step).wait_send()

    @pl.loop(0, STAGES)
    def _(stage):
        for way in range(2):
            @pl.when(stage < STAGES - 2)
            def _():
                chunk_copy(held.at[0, 0], 0, 0, ring_send.at[way, 2 + stage], right).wait_send()

            chunk_copy(held.at[0, 0], 0, 0, side_send.at[way, 2 + stage], sibling).wait_send()

    for turn in range(2):
        for way in range(2):
            chunk_copy(context.at[0], 0, 0, ring_send.at[way, turn], right).wait_send()
        chunk_copy(context.at[0], 0, 0, side_send.at[0, turn], sibling).wait_send()


def per_device(context, grad, users, counts):
    examples, length, width_in = context.shape
    width_out = grad.shape[2]
    tiles = width_out // 8
    half, quarter = tiles // 2, tiles // 4
    dma = pltpu.SemaphoreType.DMA
    vmem = pltpu.VMEM
    clip_bound = 1.5 * math.sqrt(width_in * width_out * GROUP * GROUP)
    flops = 2 * examples * length * width_in * width_out * GROUP
    result = pl.pallas_call(
        functools.partial(kernel, clip_bound),
        out_shape=jax.ShapeDtypeStruct((tiles, 8, width_in), F32),
        in_specs=[
            pl.BlockSpec(memory_space=pl.ANY),
            pl.BlockSpec(memory_space=pl.ANY),
            pl.BlockSpec(memory_space=pltpu.SMEM),
            pl.BlockSpec(memory_space=pltpu.SMEM),
        ],
        out_specs=pl.BlockSpec(memory_space=pltpu.VMEM),
        scratch_shapes=[
            vmem((GROUP, examples, length, width_in), context.dtype),
            vmem((examples, length, width_out), grad.dtype),
            vmem((examples, width_out, length), grad.dtype),
            vmem((examples, SIDE, SIDE, tiles, 8, width_in), F32),
            vmem((examples, 2 * GROUP, 8, 128), F32),
            vmem((examples, 8, width_in), F32),
            vmem((GROUP, examples, 8, 128), F32),
            vmem((GROUP, examples, 8, 128), F32),
            vmem((2, 2, 2, half, 8, width_in), F32),
            vmem((2, 2, SIDE, half, 8, width_in), F32),
            vmem((2, 2, quarter, 8, width_in), F32),
            vmem((2, 2, half, 8, width_in), F32),
            dma((2,)),
            dma((2, 2 + STAGES)),
            dma((GROUP, 2)),
            dma((2, 2 + STAGES)),
            dma((GROUP,)),
            dma((GROUP,)),
            dma((GROUP,)),
            dma((GROUP,)),
            dma((24,)),
            dma((24,)),
        ],
        compiler_params=pltpu.CompilerParams(
            collective_id=0, has_side_effects=True, vmem_limit_bytes=56 * 2**20),
        cost_estimate=pl.CostEstimate(flops=flops, bytes_accessed=2 * context.size + 2 * grad.size, transcendentals=0),
    )(context, grad, users, counts)
    return result.reshape(width_out, width_in).T


def solution(mesh):
    in_specs = (P("dp", None, "tensor"), P("dp", None, "tensor"), P(), P())
    out_specs = P("dp", "tensor")
    return jax.shard_map(
        per_device, mesh=mesh, in_specs=in_specs, out_specs=out_specs, check_vma=False
    )
```

time: 356 us -> 142 us (0.40)
  waiting for transfers between devices: 255 us -> 0 us
  Pallas kernels: 0 us -> 137 us
  blocking collectives: 56.2 us -> 0 us
  matrix products: 29.7 us -> 0 us
  between operations: 13.1 us -> 0.01 us
    reduce_scatter x2 -> x0, waiting for transfers between devices: 147 us -> none  [the longest x1 84.3 us: per_device(): lax.psum_scatter(jnp.sum(example_weight[:, None, None] * block_terms, axi...]
    pallas_call x0 -> x1, Pallas kernels: none -> 137 us  [per_device(): pl.pallas_call(functools.partial(kernel, clip_bound), out_shape=jax.Shape...]
    all_gather x1 -> x0, waiting for transfers between devices: 107 us -> none  [per_device(): gathered = lax.all_gather(context, 'tensor', axis=2, tiled=True)]
    psum x2 -> x0, blocking collectives: 56.2 us -> none  [the longest x1 33.1 us: per_device(): user_norm = lax.psum(user_local, 'dp')]
    dot_general x3 -> x0, matrix products: 29.7 us -> none  [the longest x1 14 us: per_device(): jnp.einsum('etk,etn->ekn', gathered, out_grad, preferred_element_type=jnp...]
  transfers between devices with their start and end apart: 3 -> 0, of which waited for: 3 -> 0; matrix products, arithmetic and copies ran while one was open for 0% -> 0% of each run, Pallas kernels for 0% -> 0%
where the time goes in v1:
time: 142 us; the launch traced here: 141 us
  Pallas kernels  137 us (96%)
  local copies, waits for them, and re-layouts  4.23 us (3%)
    pallas_call x1, Pallas kernels, per_device(): pl.pallas_call(functools.partial(kernel, clip_bound), out_shape=jax.Shape...  137 us
    unnamed x2, local copies, waits for them, and re-layouts  4.23 us

profile of v1, /device:TPU:1, one launch (start us, length us, event | category | flops | bytes accessed | tf_op | source)
XLA Modules:
  0.0 141.2 jit_solution(5675014712197382960)
XLA Ops:
  0.0 2.5 %copy.5.grad = bf16[2,1024,288]{2,1,0:T(8,128)(2,1)} copy(bf16[2,1024,288]{1,2,0:T(8,128)(2,1)} %param.5) | data formatting | bytes 2359296 | tf_op args[1]
  2.5 137.0 %shard_map.46 = f32[36,8,256]{2,1,0:T(8,128)} custom-call(bf16[2,1024,256]{2,1,0:T(8,128)(2,1)} %context.1, bf16[2,1024,288]{2,1,0:T(8,128)(2,1)} %copy.5.grad, s32[32]{0:T(128)} %users.1, s32[16]{0:T(128)} %counts.1), custom_call_target="tpu_custom_call" | custom-call | flops 4831838208 | bytes 2228224 | tf_op jit(solution)/shard_map/pallas_call | solution.py:281
  139.5 1.7 %copy.7 = f32[256,288]{0,1:T(8,128)} copy(f32[256,288]{0,1:T(8,128)} %bitcast.3) | data formatting | bytes 589824

commit v2 on v1

v2 whole, which is shorter than its diff:
```python
import functools
import math

import jax
import jax.numpy as jnp
from jax import lax
from jax.experimental import pallas as pl
from jax.experimental.pallas import tpu as pltpu
from jax.sharding import PartitionSpec as P

MESH = pl.DeviceIdType.MESH
F32 = jnp.float32
SIDE = 4
RING = 8
GROUP = 16
STAGES = RING - 1
STEPS = 32000.0
FIRST_UNITS = 9


def kernel(clip_bound, context, grad, users, counts, out, held, grad_t, terms, coded_x, coded_y, early_x, early_y,
           same_user, user_count, weight, squares, square_box, norm_box, sum_x, sum_y, second_x, second_y, last_x, last_y,
           local_sem, ring_send, ring_recv, side_send, early_send, early_recv, square_send, square_recv,
           norm_send, norm_recv, sum_send, sum_recv):
    data, tensor = lax.axis_index("dp"), lax.axis_index("tensor")
    depth, core = lax.div(tensor, 2), lax.rem(tensor, 2)
    place = (lax.div(data, SIDE), lax.rem(data, SIDE))
    coded, early = (coded_x, coded_y), (early_x, early_y)
    sums, second, last = (sum_x, sum_y), (second_x, second_y), (last_x, last_y)
    units = (coded_x.shape[2] - 1, coded_y.shape[2] - 1)
    starts = (0, units[0])

    def on_ring(step):
        return lax.rem(depth + step + RING, RING)

    right = (data, on_ring(1) * 2 + core)
    left = (data, on_ring(-1) * 2 + core)
    sibling = (data, depth * 2 + 1 - core)

    load_grad = pltpu.make_async_copy(grad, grad_t, local_sem.at[0])
    load_grad.start()
    load_own = pltpu.make_async_copy(context, held.at[tensor], local_sem.at[1])
    load_own.start()

    barrier = pltpu.get_barrier_semaphore()

    @pl.loop(1, GROUP)
    def _(step):
        pl.semaphore_signal(barrier, inc=1, device_id=(data, lax.rem(tensor + step, GROUP)), device_id_type=MESH)
        pl.semaphore_signal(barrier, inc=1, device_id=(lax.rem(data + step, GROUP), tensor), device_id_type=MESH)

    pl.semaphore_wait(barrier, 2 * (GROUP - 1))

    def chunk_copy(src, slot, example, send_sem, device):
        return pltpu.make_async_remote_copy(
            src_ref=src, dst_ref=held.at[slot, example], send_sem=send_sem,
            recv_sem=ring_recv.at[slot, example], device_id=device, device_id_type=MESH)

    for turn in range(2):
        chunk_copy(context.at[turn], tensor, turn, ring_send.at[0, turn], right).start()
        chunk_copy(context.at[1 - turn], tensor, 1 - turn, ring_send.at[1, turn], left).start()
    for turn in range(2):
        chunk_copy(context.at[turn], tensor, turn, side_send.at[0, turn], sibling).start()

    squares[...] = jnp.zeros_like(squares)
    lanes = lax.broadcasted_iota(jnp.int32, (1, 128), 1)
    everyone = jnp.full((1, 128), -1, jnp.int32)
    for item in range(2 * GROUP):
        everyone = jnp.where(lanes == item, users[item], everyone)

    @pl.loop(0, 2 * GROUP)
    def _(item):
        same_user[item] = jnp.where(everyone == users[item], 1.0, 0.0)
        user_count[item] = jnp.full((1, 128), counts[users[item]].astype(F32), F32)

    load_grad.wait()

    def early_copy(part, slot, example):
        spot = (lax.div(slot, SIDE), lax.rem(slot, SIDE))
        owner = (spot[0] * SIDE + place[1], tensor) if part == 0 else (place[0] * SIDE + spot[1], tensor)
        return pltpu.make_async_remote_copy(
            src_ref=coded[part].at[slot, example], dst_ref=early[part].at[place[part], example, spot[1 - part]],
            send_sem=early_send.at[part], recv_sem=early_recv.at[part], device_id=owner, device_id_type=MESH)

    def product(slot, example):
        term = jnp.dot(grad_t[example], held[slot, example], preferred_element_type=F32)
        tiles = term.reshape(terms.shape[3:])
        spot = (lax.div(slot, SIDE), lax.rem(slot, SIDE))
        terms[example, spot[0], spot[1]] = tiles
        squares[example] += jnp.sum(tiles * tiles, axis=0)
        peak = jnp.max(jnp.max(jnp.abs(tiles), axis=0), axis=0, keepdims=True)
        power = jnp.ceil(jnp.log2(jnp.maximum(peak, 1e-30)))
        steps = jnp.round(term * (STEPS * jnp.exp2(-power))).astype(jnp.int32).astype(jnp.int16)
        steps = steps.reshape((sum(units), 16) + steps.shape[1:])
        powers = jnp.broadcast_to(power, (16,) + power.shape[1:]).astype(jnp.int32).astype(jnp.int16)
        for part in range(2):
            coded[part][slot, example, 0:units[part]] = steps[starts[part]:starts[part] + units[part]]
            coded[part][slot, example, units[part]] = powers

            @pl.when(spot[part] != place[part])
            def _():
                early_copy(part, slot, example).start()

    def arrived(slot, example):
        chunk_copy(context.at[0], slot, example, ring_send.at[0, 0], right).wait_recv()

    load_own.wait()
    for example in range(2):
        product(tensor, example)
    for example in range(2):
        arrived(depth * 2 + 1 - core, example)
        product(depth * 2 + 1 - core, example)

    @pl.loop(0, STAGES)
    def _(stage):
        distance = 1 + lax.div(stage, 2)
        turn = lax.rem(stage, 2)
        sources = ((on_ring(-distance), turn), (on_ring(distance), 1 - turn))
        for way, (source, example) in enumerate(sources):
            slot = source * 2 + core
            arrived(slot, example)

            @pl.when(stage < STAGES - 2)
            def _():
                chunk_copy(held.at[slot, example], slot, example, ring_send.at[way, 2 + stage],
                           (right, left)[way]).start()

            chunk_copy(held.at[slot, example], slot, example, side_send.at[way, 2 + stage], sibling).start()
        for source, example in sources:
            product(source * 2 + core, example)
        for source, example in sources:
            arrived(source * 2 + 1 - core, example)
            product(source * 2 + 1 - core, example)

    lanes = lax.broadcasted_iota(jnp.int32, (8, 128), 1)

    def in_lanes(values):
        return jnp.where(lanes == 2 * data, values[0], jnp.where(lanes == 2 * data + 1, values[1], 0.0))

    own = [jnp.sum(jnp.sum(squares[example], axis=1, keepdims=True), axis=0, keepdims=True) for example in range(2)]
    square_box[tensor] = in_lanes(own)

    def square_copy(step):
        return pltpu.make_async_remote_copy(
            src_ref=square_box.at[tensor], dst_ref=square_box.at[tensor], send_sem=square_send.at[step],
            recv_sem=square_recv.at[tensor], device_id=(data, lax.rem(tensor + step, GROUP)), device_id_type=MESH)

    def square_arrival(step):
        peer = lax.rem(tensor + step, GROUP)
        return pltpu.make_async_remote_copy(
            src_ref=square_box.at[peer], dst_ref=square_box.at[peer], send_sem=square_send.at[step],
            recv_sem=square_recv.at[peer], device_id=(data, peer), device_id_type=MESH)

    @pl.loop(1, GROUP)
    def _(step):
        square_copy(step).start()

    @pl.loop(1, GROUP)
    def _(step):
        square_arrival(step).wait_recv()

    norm = jnp.sqrt(jnp.sum(square_box[...], axis=0) + 1e-6)
    norm_box[data] = in_lanes((norm, norm))

    def norm_copy(step):
        return pltpu.make_async_remote_copy(
            src_ref=norm_box.at[data], dst_ref=norm_box.at[data], send_sem=norm_send.at[step],
            recv_sem=norm_recv.at[data], device_id=(lax.rem(data + step, GROUP), tensor), device_id_type=MESH)

    def norm_arrival(step):
        peer = lax.rem(data + step, GROUP)
        return pltpu.make_async_remote_copy(
            src_ref=norm_box.at[peer], dst_ref=norm_box.at[peer], send_sem=norm_send.at[step],
            recv_sem=norm_recv.at[peer], device_id=(peer, tensor), device_id_type=MESH)

    @pl.loop(1, GROUP)
    def _(step):
        norm_copy(step).start()

    @pl.loop(1, GROUP)
    def _(step):
        norm_arrival(step).wait_recv()

    norms = jnp.sum(norm_box[...], axis=0)[0:1]
    user_norm = jnp.sum(same_user[...] * norms, axis=2, keepdims=True)
    count = user_count[...]
    weight[...] = jnp.minimum(1.0, clip_bound * count / user_norm) / (count * counts.shape[0])

    def wide(row):
        return jnp.concatenate([row, row], axis=1)

    def along(dim, step):
        return lax.rem(place[dim] + step + SIDE, SIDE)

    def at(dim, value):
        return value * SIDE + place[1] if dim == 0 else place[0] * SIDE + value

    def gathered(part, other):
        spot = (place[0], other) if part == 0 else (other, place[1])
        span = pl.ds(2 * starts[part], 2 * units[part])
        total = sum(wide(weight[2 * data + example]) * terms[(example,) + spot + (span,)] for example in range(2))
        for step in range(1, SIDE):
            source = along(part, step)
            for example in range(2):
                block = early[part].at[source, example, other]
                power = block[units[part]].astype(jnp.int32).astype(F32)[0:1]
                scale = wide(weight[2 * at(part, source) + example]) * (jnp.exp2(power) * (1.0 / STEPS))
                steps = block[0:units[part]].astype(jnp.int32).astype(F32)
                total = total + scale * steps.reshape(total.shape)
        return total

    def sum_copy(part, message, way, src, dst):
        number = (part * 3 + message) * 2 + way
        dim = 1 - part
        return pltpu.make_async_remote_copy(
            src_ref=src, dst_ref=dst, send_sem=sum_send.at[number], recv_sem=sum_recv.at[number],
            device_id=(at(dim, along(dim, 1 if way == 0 else -1)), tensor), device_id_type=MESH)

    copies = []

    def send(*args):
        copy = sum_copy(*args)
        copy.start()
        copies.append(copy)
        return copy

    lows = tuple((pl.ds(0, count), pl.ds(count, count)) for count in units)
    firsts, raws, joined = {}, {}, {}
    for part in range(2):
        pltpu.make_async_remote_copy(
            src_ref=early[part].at[pl.ds(0, SIDE - 1)], dst_ref=early[part].at[pl.ds(0, SIDE - 1)],
            send_sem=early_send.at[part], recv_sem=early_recv.at[part], device_id=sibling, device_id_type=MESH).wait_recv()
    for part in range(2):
        other = along(1 - part, 2)
        sums[part][other] = gathered(part, other)
        for way in range(2):
            firsts[part, way] = send(part, 0, way, sums[part].at[other, lows[part][way]], second[part].at[way])
    for part in range(2):
        for way in range(2):
            other = along(1 - part, 1 if way == 0 else -1)
            sums[part][other] = gathered(part, other)
            span = lows[part][1 - way]
            raws[part, way] = send(part, 1, way, sums[part].at[other, span], last[part].at[way, span])
    for part in range(2):
        for way in range(2):
            other = along(1 - part, 1 if way == 0 else -1)
            span = lows[part][way]
            firsts[part, way].wait_recv()
            sums[part][other, span] = sums[part][other, span] + second[part][way]
            joined[part, way] = send(part, 2, way, sums[part].at[other, span], last[part].at[way, span])
    for part in range(2):
        sums[part][place[1 - part]] = gathered(part, place[1 - part])
    for part in range(2):
        for way in range(2):
            raws[part, way].wait_recv()
            joined[part, way].wait_recv()
        out[pl.ds(2 * starts[part], 2 * units[part])] = sums[part][place[1 - part]] + (last[part][0] + last[part][1])

    for copy in copies:
        copy.wait_send()
    for part in range(2):
        pltpu.make_async_remote_copy(
            src_ref=early[part].at[pl.ds(0, SIDE - 1)], dst_ref=early[part].at[pl.ds(0, SIDE - 1)],
            send_sem=early_send.at[part], recv_sem=early_recv.at[part], device_id=sibling, device_id_type=MESH).wait_send()

    @pl.loop(1, GROUP)
    def _(step):
        square_copy(step).wait_send()
        norm_copy(step).wait_send()

    @pl.loop(0, STAGES)
    def _(stage):
        for way in range(2):
            @pl.when(stage < STAGES - 2)
            def _():
                chunk_copy(held.at[0, 0], 0, 0, ring_send.at[way, 2 + stage], right).wait_send()

            chunk_copy(held.at[0, 0], 0, 0, side_send.at[way, 2 + stage], sibling).wait_send()

    for turn in range(2):
        for way in range(2):
            chunk_copy(context.at[0], 0, 0, ring_send.at[way, turn], right).wait_send()
        chunk_copy(context.at[0], 0, 0, side_send.at[0, turn], sibling).wait_send()


def per_device(context, grad, users, counts):
    examples, length, width_in = context.shape
    width_out = grad.shape[2]
    tiles = width_out // 8
    units = (FIRST_UNITS, width_out // 16 - FIRST_UNITS)
    dma = pltpu.SemaphoreType.DMA
    vmem = pltpu.VMEM
    clip_bound = 1.5 * math.sqrt(width_in * width_out * GROUP * GROUP)
    flops = 2 * examples * length * width_in * width_out * GROUP
    result = pl.pallas_call(
        functools.partial(kernel, clip_bound),
        out_shape=jax.ShapeDtypeStruct((tiles, 8, width_in), F32),
        in_specs=[
            pl.BlockSpec(memory_space=pl.ANY),
            pl.BlockSpec(memory_space=pl.ANY),
            pl.BlockSpec(memory_space=pltpu.SMEM),
            pl.BlockSpec(memory_space=pltpu.SMEM),
        ],
        out_specs=pl.BlockSpec(memory_space=pltpu.VMEM),
        scratch_shapes=[
            vmem((GROUP, examples, length, width_in), context.dtype),
            vmem((examples, width_out, length), grad.dtype),
            vmem((examples, SIDE, SIDE, tiles, 8, width_in), F32),
            *(vmem((GROUP, examples, count + 1, 16, width_in), jnp.int16) for count in units),
            *(vmem((SIDE, examples, SIDE, count + 1, 16, width_in), jnp.int16) for count in units),
            vmem((2 * GROUP, 1, 128), F32),
            vmem((2 * GROUP, 1, 128), F32),
            vmem((2 * GROUP, 1, 128), F32),
            vmem((examples, 8, width_in), F32),
            vmem((GROUP, 8, 128), F32),
            vmem((GROUP, 8, 128), F32),
            *(vmem((SIDE, 2 * count, 8, width_in), F32) for count in units),
            *(vmem((2, count, 8, width_in), F32) for count in units),
            *(vmem((2, 2 * count, 8, width_in), F32) for count in units),
            dma((2,)),
            dma((2, 2 + STAGES)),
            dma((GROUP, 2)),
            dma((2, 2 + STAGES)),
            dma((2,)),
            dma((2,)),
            dma((GROUP,)),
            dma((GROUP,)),
            dma((GROUP,)),
            dma((GROUP,)),
            dma((12,)),
            dma((12,)),
        ],
        compiler_params=pltpu.CompilerParams(
            collective_id=0, has_side_effects=True, vmem_limit_bytes=56 * 2**20),
        cost_estimate=pl.CostEstimate(flops=flops, bytes_accessed=2 * context.size + 2 * grad.size, transcendentals=0),
    )(context, jnp.swapaxes(grad, 1, 2), users, counts)
    return result.reshape(width_out, width_in).T


def solution(mesh):
    in_specs = (P("dp", None, "tensor"), P("dp", None, "tensor"), P(), P())
    out_specs = P("dp", "tensor")
    return jax.shard_map(
        per_device, mesh=mesh, in_specs=in_specs, out_specs=out_specs, check_vma=False
    )
```

time: 142 us -> 121 us (0.85)
  Pallas kernels: 137 us -> 118 us
  local copies, waits for them, and re-layouts: 4.23 us -> 1.69 us
    pallas_call x1, Pallas kernels: 137 us -> 118 us  [per_device(): pl.pallas_call(functools.partial(kernel, clip_bound), out_shape=jax.Shape...]
    unnamed x2 -> x1, local copies, waits for them, and re-layouts: 4.23 us -> 1.69 us
where the time goes in v2:
time: 121 us; the launch traced here: 120 us
  Pallas kernels  118 us (98%)
  local copies, waits for them, and re-layouts  1.69 us (1%)
    pallas_call x1, Pallas kernels, per_device(): pl.pallas_call(functools.partial(kernel, clip_bound), out_shape=jax.Shape...  118 us

profile of v2, /device:TPU:1, one launch (start us, length us, event | category | flops | bytes accessed | tf_op | source)
XLA Modules:
  0.0 119.6 jit_solution(9082413101220274284)
XLA Ops:
  0.0 117.9 %shard_map.46 = f32[36,8,256]{2,1,0:T(8,128)} custom-call(bf16[2,1024,256]{2,1,0:T(8,128)(2,1)} %context.1, bf16[2,288,1024]{2,1,0:T(8,128)(2,1)} %bitcast.5, s32[32]{0:T(128)} %users.1, s32[16]{0:T(128)} %counts.1), custom_call_target="tpu_custom_call" | custom-call | flops 4831838208 | bytes 2228224 | tf_op jit(solution)/shard_map/pallas_call | solution.py:295
  117.9 1.7 %copy.6 = f32[256,288]{0,1:T(8,128)} copy(f32[256,288]{0,1:T(8,128)} %bitcast.4) | data formatting | bytes 589824

commit v3 on v0

v3 whole, which is shorter than its diff:
```python
import functools
import math

import jax
import jax.numpy as jnp
from jax import lax
from jax.experimental import pallas as pl
from jax.experimental.pallas import tpu as pltpu
from jax.sharding import PartitionSpec as P

MESH = pl.DeviceIdType.MESH
F32 = jnp.float32
SIDE = 4
RING = 8
GROUP = 16
LANES = 128
HALVES = 2
PIECES = 2 * HALVES
STAGES = (RING // 2 - 1) * PIECES + HALVES
FORWARDS = STAGES - PIECES
STEPS = 32000.0
FIRST_UNITS = 9
FAR_TENSOR = sorted(range(1, GROUP), key=lambda step: -min(step, GROUP - step))
FAR_DATA = sorted(range(1, GROUP), key=lambda step: -min(step // SIDE, SIDE - step // SIDE) - min(step % SIDE, SIDE - step % SIDE))


def encode(tiles):
    peak = jnp.max(jnp.max(jnp.abs(tiles), axis=0), axis=0, keepdims=True)
    power = jnp.ceil(jnp.log2(jnp.maximum(peak, 1e-30)))
    steps = jnp.round(tiles * (STEPS * jnp.exp2(-power))[None]).astype(jnp.int32).astype(jnp.int16)
    powers = jnp.broadcast_to(power, (16,) + power.shape[1:]).astype(jnp.int32).astype(jnp.int16)
    return steps.reshape((tiles.shape[0] // 2, 16) + tiles.shape[2:]), powers


def decode(ref, factor):
    units = ref.shape[0] - 1
    power = ref[units].astype(jnp.int32).astype(F32)[0:1]
    scale = factor * (jnp.exp2(power) * (1.0 / STEPS))
    steps = ref[0:units].astype(jnp.int32).astype(F32)
    return scale * steps.reshape((2 * units, 8) + ref.shape[2:])


def kernel(clip_bound, context, grad, users, counts, out, held, grad_t, terms, coded_x, coded_y, early_x, early_y,
           same_user, user_count, weight, squares, square_box, norm_box, late_x, late_y, final_x, final_y,
           local_sem, ring_send, ring_recv, side_send, early_send, early_recv, square_send, square_recv,
           norm_send, norm_recv, sum_send, sum_recv, hello):
    data, tensor = lax.axis_index("dp"), lax.axis_index("tensor")
    depth, core = lax.div(tensor, 2), lax.rem(tensor, 2)
    place = (lax.div(data, SIDE), lax.rem(data, SIDE))
    coded, early = (coded_x, coded_y), (early_x, early_y)
    late, final = (late_x, late_y), (final_x, final_y)
    units = (coded_x.shape[3] - 1, coded_y.shape[3] - 1)
    starts = (0, units[0])

    def on_ring(step):
        return lax.rem(depth + step + RING, RING)

    def along(dim, step):
        return lax.rem(place[dim] + step + SIDE, SIDE)

    def at(dim, value):
        return value * SIDE + place[1] if dim == 0 else place[0] * SIDE + value

    right = (data, on_ring(1) * 2 + core)
    left = (data, on_ring(-1) * 2 + core)
    sibling = (data, depth * 2 + 1 - core)
    around = tuple((at(dim, along(dim, step)), tensor) for dim in range(2) for step in (1, -1))

    barrier = pltpu.get_barrier_semaphore()
    for device in (right, left) + around + (sibling,):
        pl.semaphore_signal(barrier, inc=1, device_id=device, device_id_type=MESH)

    load_grad = pltpu.make_async_copy(grad, grad_t, local_sem.at[0])
    loads = []
    for example in range(2):
        for part in range(HALVES):
            loads.append(pltpu.make_async_copy(
                context.at[example, :, pl.ds(part * LANES, LANES)], held.at[tensor, example, part],
                local_sem.at[1 + example * HALVES + part]))
    for copy in loads:
        copy.start()
    load_grad.start()
    for copy in loads:
        copy.wait()

    pl.semaphore_wait(barrier, 7)

    def chunk_copy(slot, example, part, send_sem, device):
        return pltpu.make_async_remote_copy(
            src_ref=held.at[slot, example, part], dst_ref=held.at[slot, example, part], send_sem=send_sem,
            recv_sem=ring_recv.at[slot, example, part], device_id=device, device_id_type=MESH)

    for piece in range(PIECES):
        turn, part = piece // HALVES, piece % HALVES
        chunk_copy(tensor, turn, part, ring_send.at[0, piece], right).start()
        chunk_copy(tensor, 1 - turn, part, ring_send.at[1, piece], left).start()
    for piece in range(PIECES):
        chunk_copy(tensor, piece // HALVES, piece % HALVES, side_send.at[0, piece], sibling).start()

    for turn in range(3):
        for device in around:
            pl.semaphore_signal(hello.at[turn], inc=1, device_id=device, device_id_type=MESH)
        pl.semaphore_wait(hello.at[turn], 4)

    squares[...] = jnp.zeros_like(squares)
    lanes = lax.broadcasted_iota(jnp.int32, (1, LANES), 1)
    everyone = jnp.full((1, LANES), -1, jnp.int32)
    for item in range(2 * GROUP):
        everyone = jnp.where(lanes == item, users[item], everyone)

    @pl.loop(0, 2 * GROUP)
    def _(item):
        same_user[item] = jnp.where(everyone == users[item], 1.0, 0.0)
        user_count[item] = jnp.full((1, LANES), counts[users[item]].astype(F32), F32)

    load_grad.wait()

    def early_copy(dim, slot, example, part):
        spot = (lax.div(slot, SIDE), lax.rem(slot, SIDE))
        return pltpu.make_async_remote_copy(
            src_ref=coded[dim].at[slot, example, part], dst_ref=early[dim].at[place[dim], example, spot[1 - dim], part],
            send_sem=early_send.at[dim], recv_sem=early_recv.at[dim], device_id=(at(dim, spot[dim]), tensor),
            device_id_type=MESH)

    def product(slot, example, part):
        term = jnp.dot(grad_t[example], held[slot, example, part], preferred_element_type=F32)
        tiles = term.reshape(terms.shape[4:])
        spot = (lax.div(slot, SIDE), lax.rem(slot, SIDE))
        terms[example, spot[0], spot[1], part] = tiles
        squares[example] += jnp.sum(tiles * tiles, axis=0)
        steps, powers = encode(tiles)
        for dim in range(2):
            coded[dim][slot, example, part, 0:units[dim]] = steps[starts[dim]:starts[dim] + units[dim]]
            coded[dim][slot, example, part, units[dim]] = powers

            @pl.when(spot[dim] != place[dim])
            def _():
                early_copy(dim, slot, example, part).start()

    def arrived(slot, example, part):
        chunk_copy(slot, example, part, ring_send.at[0, 0], right).wait_recv()

    @pl.loop(0, PIECES)
    def _(piece):
        product(tensor, lax.div(piece, HALVES), lax.rem(piece, HALVES))

    @pl.loop(0, PIECES)
    def _(piece):
        example, part = lax.div(piece, HALVES), lax.rem(piece, HALVES)
        arrived(depth * 2 + 1 - core, example, part)
        product(depth * 2 + 1 - core, example, part)

    @pl.loop(0, STAGES)
    def _(stage):
        distance = 1 + lax.div(stage, PIECES)
        turn = lax.div(lax.rem(stage, PIECES), HALVES)
        part = lax.rem(stage, HALVES)
        sources = ((on_ring(-distance), turn), (on_ring(distance), 1 - turn))
        for way, (source, example) in enumerate(sources):
            slot = source * 2 + core
            arrived(slot, example, part)

            @pl.when(stage < FORWARDS)
            def _():
                chunk_copy(slot, example, part, ring_send.at[way, PIECES + stage], (right, left)[way]).start()

            chunk_copy(slot, example, part, side_send.at[way, PIECES + stage], sibling).start()
        for source, example in sources:
            product(source * 2 + core, example, part)
        for source, example in sources:
            arrived(source * 2 + 1 - core, example, part)
            product(source * 2 + 1 - core, example, part)

    lanes = lax.broadcasted_iota(jnp.int32, (8, LANES), 1)

    def in_lanes(values):
        return jnp.where(lanes == 2 * data, values[0], jnp.where(lanes == 2 * data + 1, values[1], 0.0))

    own = [jnp.sum(jnp.sum(squares[example], axis=0, keepdims=True), axis=1, keepdims=True) for example in range(2)]
    square_box[tensor] = in_lanes(own)

    def square_copy(step, index):
        return pltpu.make_async_remote_copy(
            src_ref=square_box.at[tensor], dst_ref=square_box.at[tensor], send_sem=square_send.at[step],
            recv_sem=square_recv.at[index], device_id=(data, lax.rem(tensor + step, GROUP)), device_id_type=MESH)

    for step in FAR_TENSOR:
        square_copy(step, tensor).start()
    for step in reversed(FAR_TENSOR):
        square_copy(step, lax.rem(tensor + step, GROUP)).wait_recv()

    norm = jnp.sqrt(jnp.sum(square_box[...], axis=0) + 1e-6)
    norm_box[data] = in_lanes((norm, norm))

    def norm_copy(step, index):
        peer = lax.rem(place[0] + step // SIDE, SIDE) * SIDE + lax.rem(place[1] + step % SIDE, SIDE)
        return pltpu.make_async_remote_copy(
            src_ref=norm_box.at[data], dst_ref=norm_box.at[data], send_sem=norm_send.at[step],
            recv_sem=norm_recv.at[peer if index is None else index], device_id=(peer, tensor), device_id_type=MESH)

    for step in FAR_DATA:
        norm_copy(step, data).start()
    for step in reversed(FAR_DATA):
        norm_copy(step, None).wait_recv()

    norms = jnp.sum(norm_box[...], axis=0)[0:1]
    user_norm = jnp.sum(same_user[...] * norms, axis=2, keepdims=True)
    count = user_count[...]
    weight[...] = jnp.minimum(1.0, clip_bound * count / user_norm) / (count * counts.shape[0])

    def all_early(dim):
        whole = early[dim].at[pl.ds(0, SIDE - 1)]
        return pltpu.make_async_remote_copy(
            src_ref=whole, dst_ref=whole, send_sem=early_send.at[dim], recv_sem=early_recv.at[dim],
            device_id=sibling, device_id_type=MESH)

    def gathered(dim, other, part):
        spot = (place[0], other) if dim == 0 else (other, place[1])
        span = pl.ds(2 * starts[dim], 2 * units[dim])
        total = sum(weight[2 * data + example] * terms[(example,) + spot + (part, span)] for example in range(2))
        for step in range(1, SIDE):
            source = along(dim, step)
            for example in range(2):
                total = total + decode(early[dim].at[source, example, other, part], weight[2 * at(dim, source) + example])
        return total

    def sum_copy(dim, step):
        return pltpu.make_async_remote_copy(
            src_ref=late[dim].at[step - 1], dst_ref=final[dim].at[step - 1], send_sem=sum_send.at[dim, step - 1],
            recv_sem=sum_recv.at[dim, step - 1], device_id=(at(1 - dim, along(1 - dim, step)), tensor),
            device_id_type=MESH)

    for dim in range(2):
        all_early(dim).wait_recv()
    for step in (2, 1, 3):
        for dim in range(2):
            for part in range(HALVES):
                steps, powers = encode(gathered(dim, along(1 - dim, step), part))
                late[dim][step - 1, part, 0:units[dim]] = steps
                late[dim][step - 1, part, units[dim]] = powers
            sum_copy(dim, step).start()
    own = {}
    for dim in range(2):
        for part in range(HALVES):
            span = pl.ds(2 * starts[dim], 2 * units[dim])
            out[span, :, pl.ds(part * LANES, LANES)] = gathered(dim, place[1 - dim], part)
    for step in (1, 3, 2):
        for dim in range(2):
            sum_copy(dim, step).wait_recv()
            for part in range(HALVES):
                span = pl.ds(2 * starts[dim], 2 * units[dim])
                out[span, :, pl.ds(part * LANES, LANES)] += decode(final[dim].at[step - 1, part], 1.0)

    for dim in range(2):
        for step in range(1, SIDE):
            sum_copy(dim, step).wait_send()
        all_early(dim).wait_send()
    for step in range(1, GROUP):
        square_copy(step, tensor).wait_send()
        norm_copy(step, data).wait_send()

    @pl.loop(0, PIECES + STAGES)
    def _(index):
        for way in range(2):
            @pl.when(index < PIECES + FORWARDS)
            def _():
                chunk_copy(0, 0, 0, ring_send.at[way, index], right).wait_send()

            if way == 0:
                chunk_copy(0, 0, 0, side_send.at[way, index], sibling).wait_send()
            else:
                @pl.when(index >= PIECES)
                def _():
                    chunk_copy(0, 0, 0, side_send.at[way, index], sibling).wait_send()


def per_device(context, grad, users, counts):
    examples, length, width_in = context.shape
    width_out = grad.shape[2]
    tiles = width_out // 8
    units = (FIRST_UNITS, width_out // 16 - FIRST_UNITS)
    dma = pltpu.SemaphoreType.DMA
    vmem = pltpu.VMEM
    int16 = jnp.int16
    clip_bound = 1.5 * math.sqrt(width_in * width_out * GROUP * GROUP)
    flops = 2 * examples * length * width_in * width_out * GROUP
    result = pl.pallas_call(
        functools.partial(kernel, clip_bound),
        out_shape=jax.ShapeDtypeStruct((tiles, 8, width_in), F32),
        in_specs=[
            pl.BlockSpec(memory_space=pl.ANY),
            pl.BlockSpec(memory_space=pl.ANY),
            pl.BlockSpec(memory_space=pltpu.SMEM),
            pl.BlockSpec(memory_space=pltpu.SMEM),
        ],
        out_specs=pl.BlockSpec(memory_space=pltpu.VMEM),
        scratch_shapes=[
            vmem((GROUP, examples, HALVES, length, LANES), context.dtype),
            vmem((examples, width_out, length), grad.dtype),
            vmem((examples, SIDE, SIDE, HALVES, tiles, 8, LANES), F32),
            *(vmem((GROUP, examples, HALVES, count + 1, 16, LANES), int16) for count in units),
            *(vmem((SIDE, examples, SIDE, HALVES, count + 1, 16, LANES), int16) for count in units),
            vmem((2 * GROUP, 1, LANES), F32),
            vmem((2 * GROUP, 1, LANES), F32),
            vmem((2 * GROUP, 1, LANES), F32),
            vmem((examples, 8, LANES), F32),
            vmem((GROUP, 8, LANES), F32),
            vmem((GROUP, 8, LANES), F32),
            *(vmem((SIDE - 1, HALVES, count + 1, 16, LANES), int16) for count in units),
            *(vmem((SIDE - 1, HALVES, count + 1, 16, LANES), int16) for count in units),
            dma((1 + PIECES,)),
            dma((2, PIECES + STAGES)),
            dma((GROUP, 2, HALVES)),
            dma((2, PIECES + STAGES)),
            dma((2,)),
            dma((2,)),
            dma((GROUP,)),
            dma((GROUP,)),
            dma((GROUP,)),
            dma((GROUP,)),
            dma((2, SIDE - 1)),
            dma((2, SIDE - 1)),
            pltpu.SemaphoreType.REGULAR((3,)),
        ],
        compiler_params=pltpu.CompilerParams(
            collective_id=0, has_side_effects=True, vmem_limit_bytes=56 * 2**20),
        cost_estimate=pl.CostEstimate(flops=flops, bytes_accessed=2 * context.size + 2 * grad.size, transcendentals=0),
    )(context, jnp.swapaxes(grad, 1, 2), users, counts)
    return result.reshape(width_out, width_in).T


def solution(mesh):
    in_specs = (P("dp", None, "tensor"), P("dp", None, "tensor"), P(), P())
    out_specs = P("dp", "tensor")
    return jax.shard_map(
        per_device, mesh=mesh, in_specs=in_specs, out_specs=out_specs, check_vma=False
    )
```

time: 356 us -> 112 us (0.31)
  waiting for transfers between devices: 255 us -> 0 us
  Pallas kernels: 0 us -> 110 us
  blocking collectives: 56.2 us -> 0 us
  matrix products: 29.7 us -> 0 us
  between operations: 13.1 us -> 0.01 us
    reduce_scatter x2 -> x0, waiting for transfers between devices: 147 us -> none  [the longest x1 84.3 us: per_device(): lax.psum_scatter(jnp.sum(example_weight[:, None, None] * block_terms, axi...]
    pallas_call x0 -> x1, Pallas kernels: none -> 110 us  [per_device(): pl.pallas_call(functools.partial(kernel, clip_bound), out_shape=jax.Shape...]
    all_gather x1 -> x0, waiting for transfers between devices: 107 us -> none  [per_device(): gathered = lax.all_gather(context, 'tensor', axis=2, tiled=True)]
    psum x2 -> x0, blocking collectives: 56.2 us -> none  [the longest x1 33.1 us: per_device(): user_norm = lax.psum(user_local, 'dp')]
    dot_general x3 -> x0, matrix products: 29.7 us -> none  [the longest x1 14 us: per_device(): jnp.einsum('etk,etn->ekn', gathered, out_grad, preferred_element_type=jnp...]
  transfers between devices with their start and end apart: 3 -> 0, of which waited for: 3 -> 0; matrix products, arithmetic and copies ran while one was open for 0% -> 0% of each run, Pallas kernels for 0% -> 0%
where the time goes in v3:
time: 112 us
  Pallas kernels  110 us (98%)
  local copies, waits for them, and re-layouts  1.69 us (2%)
    pallas_call x1, Pallas kernels, per_device(): pl.pallas_call(functools.partial(kernel, clip_bound), out_shape=jax.Shape...  110 us

profile of v3, /device:TPU:1, one launch (start us, length us, event | category | flops | bytes accessed | tf_op | source)
XLA Modules:
  0.0 111.6 jit_solution(9368220477037093539)
XLA Ops:
  0.0 109.9 %shard_map.46 = f32[36,8,256]{2,1,0:T(8,128)} custom-call(bf16[2,1024,256]{2,1,0:T(8,128)(2,1)} %context.1, bf16[2,288,1024]{2,1,0:T(8,128)(2,1)} %bitcast.5, s32[32]{0:T(128)} %users.1, s32[16]{0:T(128)} %counts.1), custom_call_target="tpu_custom_call" | custom-call | flops 4831838208 | bytes 2228224 | tf_op jit(solution)/shard_map/pallas_call | solution.py:287
  109.9 1.7 %copy.6 = f32[256,288]{0,1:T(8,128)} copy(f32[256,288]{0,1:T(8,128)} %bitcast.4) | data formatting | bytes 589824

commit v4 on v3

--- a/solution.py
+++ b/solution.py
@@ -186,6 +186,20 @@
 
     for step in FAR_TENSOR:
         square_copy(step, tensor).start()
+    @pl.loop(0, PIECES + STAGES)
+    def _(index):
+        for way in range(2):
+            @pl.when(index < PIECES + FORWARDS)
+            def _():
+                chunk_copy(0, 0, 0, ring_send.at[way, index], right).wait_send()
+
+            if way == 0:
+                chunk_copy(0, 0, 0, side_send.at[way, index], sibling).wait_send()
+            else:
+                @pl.when(index >= PIECES)
+                def _():
+                    chunk_copy(0, 0, 0, side_send.at[way, index], sibling).wait_send()
+
     for step in reversed(FAR_TENSOR):
         square_copy(step, lax.rem(tensor + step, GROUP)).wait_recv()
 
@@ -200,6 +214,8 @@
 
     for step in FAR_DATA:
         norm_copy(step, data).start()
+    for step in range(1, GROUP):
+        square_copy(step, tensor).wait_send()
     for step in reversed(FAR_DATA):
         norm_copy(step, None).wait_recv()
 
@@ -239,7 +255,10 @@
                 late[dim][step - 1, part, 0:units[dim]] = steps
                 late[dim][step - 1, part, units[dim]] = powers
             sum_copy(dim, step).start()
-    own = {}
+    for dim in range(2):
+        all_early(dim).wait_send()
+    for step in range(1, GROUP):
+        norm_copy(step, data).wait_send()
     for dim in range(2):
         for part in range(HALVES):
             span = pl.ds(2 * starts[dim], 2 * units[dim])
@@ -254,24 +273,6 @@
     for dim in range(2):
         for step in range(1, SIDE):
             sum_copy(dim, step).wait_send()
-        all_early(dim).wait_send()
-    for step in range(1, GROUP):
-        square_copy(step, tensor).wait_send()
-        norm_copy(step, data).wait_send()
-
-    @pl.loop(0, PIECES + STAGES)
-    def _(index):
-        for way in range(2):
-            @pl.when(index < PIECES + FORWARDS)
-            def _():
-                chunk_copy(0, 0, 0, ring_send.at[way, index], right).wait_send()
-
-            if way == 0:
-                chunk_copy(0, 0, 0, side_send.at[way, index], sibling).wait_send()
-            else:
-                @pl.when(index >= PIECES)
-                def _():
-                    chunk_copy(0, 0, 0, side_send.at[way, index], sibling).wait_send()
 
 
 def per_device(context, grad, users, counts):
@@ -286,7 +287,7 @@
     flops = 2 * examples * length * width_in * width_out * GROUP
     result = pl.pallas_call(
         functools.partial(kernel, clip_bound),
-        out_shape=jax.ShapeDtypeStruct((tiles, 8, width_in), F32),
+        out_shape=vmem((tiles, 8, width_in), F32),
         in_specs=[
             pl.BlockSpec(memory_space=pl.ANY),
             pl.BlockSpec(memory_space=pl.ANY),

time: 112 us -> 110 us (0.982)
  no operation moved by 1% of the time
where the time goes in v4:
time: 110 us
  Pallas kernels  109 us (99%)
    pallas_call x1, Pallas kernels, per_device(): pl.pallas_call(functools.partial(kernel, clip_bound), out_shape=vmem((til...  109 us

profile of v4, /device:TPU:1, one launch (start us, length us, event | category | flops | bytes accessed | tf_op | source)
XLA Modules:
  0.0 109.6 jit_solution(10975690195370146246)
XLA Ops:
  0.0 108.9 %shard_map.46 = f32[36,8,256]{2,1,0:T(8,128)S(1)} custom-call(bf16[2,1024,256]{2,1,0:T(8,128)(2,1)} %context.1, bf16[2,288,1024]{2,1,0:T(8,128)(2,1)} %bitcast.5, s32[32]{0:T(128)} %users.1, s32[16]{0:T(128)} %counts.1), custom_call_target="tpu_custom_call" | custom-call | flops 4831838208 | bytes 2228224 | tf_op jit(solution)/shard_map/pallas_call | solution.py:288
  108.9 0.7 copy.6

commit v5 on v4

v5 whole, which is shorter than its diff:
```python
import functools
import math

import jax
import jax.numpy as jnp
from jax import lax
from jax.experimental import pallas as pl
from jax.experimental.pallas import tpu as pltpu
from jax.sharding import PartitionSpec as P

MESH = pl.DeviceIdType.MESH
F32 = jnp.float32
SIDE = 4
RING = 8
GROUP = 16
LANES = 128
HALVES = 2
PIECES = 2 * HALVES
SIDE_SENDS = 6 * PIECES
STEPS = 32000.0
FAR_TENSOR = sorted(range(1, GROUP), key=lambda step: -min(step, GROUP - step))
FAR_DATA = sorted(range(1, GROUP), key=lambda step: -min(step // SIDE, SIDE - step // SIDE) - min(step % SIDE, SIDE - step % SIDE))


def encode(tiles):
    peak = jnp.max(jnp.max(jnp.abs(tiles), axis=0), axis=0, keepdims=True)
    power = jnp.ceil(jnp.log2(jnp.maximum(peak, 1e-30)))
    steps = jnp.round(tiles * (STEPS * jnp.exp2(-power))[None]).astype(jnp.int32).astype(jnp.int16)
    powers = jnp.broadcast_to(power, (16,) + power.shape[1:]).astype(jnp.int32).astype(jnp.int16)
    return steps.reshape((tiles.shape[0] // 2, 16) + tiles.shape[2:]), powers


def decode(ref, factor):
    units = ref.shape[0] - 1
    power = ref[units].astype(jnp.int32).astype(F32)[0:1]
    scale = factor * (jnp.exp2(power) * (1.0 / STEPS))
    steps = ref[0:units].astype(jnp.int32).astype(F32)
    return scale * steps.reshape((2 * units, 8) + ref.shape[2:])


def kernel(clip_bound, context, grad, users, counts, out, held, grad_own, grad_far, coded, early_x, early_y, late, final,
           same_user, user_count, weight, squares, square_box, norm_box,
           local_sem, ring_recv, far_send, near_send, side_send, grad_send, grad_recv, early_send, early_recv,
           square_send, square_recv, norm_send, norm_recv, total_send, total_recv, hello):
    data, tensor = lax.axis_index("dp"), lax.axis_index("tensor")
    depth, core = lax.div(tensor, 2), lax.rem(tensor, 2)
    place = (lax.div(data, SIDE), lax.rem(data, SIDE))
    units = coded.shape[4] - 1
    early = (early_x, early_y)
    rows = 16 * units
    away = 1 - 2 * lax.rem(depth, 2)

    def plane(step):
        return lax.rem(depth + away * step + RING, RING)

    def along(dim, step):
        return lax.rem(place[dim] + step + SIDE, SIDE)

    def at(dim, value):
        return value * SIDE + place[1] if dim == 0 else place[0] * SIDE + value

    far = (data, plane(1) * 2 + core)
    near = (data, plane(-1) * 2 + core)
    sibling = (data, depth * 2 + 1 - core)
    around = tuple((at(dim, along(dim, step)), tensor) for dim in range(2) for step in (1, -1))

    barrier = pltpu.get_barrier_semaphore()
    for device in (far, near) + around + (sibling,):
        pl.semaphore_signal(barrier, inc=1, device_id=device, device_id_type=MESH)

    loads = []
    for example in range(2):
        for part in range(HALVES):
            number = example * HALVES + part
            loads.append(pltpu.make_async_copy(
                grad.at[example, pl.ds(part * rows, rows)], grad_own.at[example, part], local_sem.at[number]))
            loads.append(pltpu.make_async_copy(
                context.at[example, :, pl.ds(part * LANES, LANES)], held.at[tensor, example, part],
                local_sem.at[PIECES + number]))
    for copy in loads:
        copy.start()
    for copy in loads:
        copy.wait()

    pl.semaphore_wait(barrier, 7)

    def chunk_copy(slot, example, part, send_sem, device):
        return pltpu.make_async_remote_copy(
            src_ref=held.at[slot, example, part], dst_ref=held.at[slot, example, part], send_sem=send_sem,
            recv_sem=ring_recv.at[slot, example, part], device_id=device, device_id_type=MESH)

    def grad_copy(example, part):
        return pltpu.make_async_remote_copy(
            src_ref=grad_own.at[example, part], dst_ref=grad_far.at[example, part],
            send_sem=grad_send.at[example, part], recv_sem=grad_recv.at[example, part],
            device_id=near, device_id_type=MESH)

    for part in range(HALVES):
        grad_copy(0, part).start()
        chunk_copy(tensor, 0, part, far_send.at[part], far).start()
    for piece in range(PIECES):
        example, part = piece // HALVES, piece % HALVES
        chunk_copy(tensor, example, part, near_send.at[piece], near).start()
        if example == 1:
            chunk_copy(tensor, example, part, far_send.at[piece], far).start()
    for piece in range(PIECES):
        chunk_copy(tensor, piece // HALVES, piece % HALVES, side_send.at[piece], sibling).start()

    for turn in range(3):
        for device in around:
            pl.semaphore_signal(hello.at[turn], inc=1, device_id=device, device_id_type=MESH)
        pl.semaphore_wait(hello.at[turn], 4)

    squares[...] = jnp.zeros_like(squares)
    lanes = lax.broadcasted_iota(jnp.int32, (1, LANES), 1)
    everyone = jnp.full((1, LANES), -1, jnp.int32)
    for item in range(2 * GROUP):
        everyone = jnp.where(lanes == item, users[item], everyone)

    @pl.loop(0, 2 * GROUP)
    def _(item):
        same_user[item] = jnp.where(everyone == users[item], 1.0, 0.0)
        user_count[item] = jnp.full((1, LANES), counts[users[item]].astype(F32), F32)

    missing = lax.rem(lax.div(depth, 2) + 2, SIDE)

    def swap(main, other):
        moved = lax.rem(missing + other, SIDE)
        return jnp.where(main == missing, moved, jnp.where(main == moved, missing, main))

    def product(lhs, slot, example, part, tile):
        lhs = lhs.reshape((2 * rows, lhs.shape[2]))
        term = jnp.dot(lhs, held[slot, example, part], preferred_element_type=F32)
        tiles = term.reshape((4 * units, 8, LANES))
        squares[example] += jnp.sum(tiles * tiles, axis=0)
        main, other = lax.div(tile, SIDE), lax.rem(tile, SIDE)
        for half in range(2):
            steps, powers = encode(tiles[2 * units * half:2 * units * (half + 1)])
            coded[tile, example, part, half, 0:units] = steps
            coded[tile, example, part, half, units] = powers
            owner = swap(main, other) if half == 0 else other

            @pl.when(owner != place[half])
            def _():
                pltpu.make_async_remote_copy(
                    src_ref=coded.at[tile, example, part, half],
                    dst_ref=early[half].at[place[half], example, (other, main)[half], part],
                    send_sem=early_send.at[half], recv_sem=early_recv.at[half],
                    device_id=(at(half, owner), tensor), device_id_type=MESH).start()

    def own_product(slot, example, part):
        product(grad_own[example], slot, example, part, slot)

    def far_product(slot, example, part):
        product(grad_far[example], slot, example, part, lax.rem(slot + 4 * away + 2 * RING, 2 * RING))

    def arrived(slot, example, part):
        chunk_copy(slot, example, part, side_send.at[0], sibling).wait_recv()

    def split(piece):
        return lax.div(piece, HALVES), lax.rem(piece, HALVES)

    @pl.loop(0, PIECES)
    def _(piece):
        own_product(tensor, *split(piece))

    @pl.loop(0, PIECES)
    def _(piece):
        arrived(depth * 2 + 1 - core, *split(piece))
        own_product(depth * 2 + 1 - core, *split(piece))

    @pl.loop(0, PIECES)
    def _(piece):
        example, part = split(piece)
        for block, device, send_sem, side in (
                (plane(1), near, near_send.at[PIECES + piece], PIECES), (plane(-1), far, far_send.at[PIECES + piece], 2 * PIECES)):
            slot = block * 2 + core
            arrived(slot, example, part)
            chunk_copy(slot, example, part, send_sem, device).start()
            chunk_copy(slot, example, part, side_send.at[side + piece], sibling).start()
        for block in (plane(1), plane(-1)):
            own_product(block * 2 + core, example, part)
        for block in (plane(1), plane(-1)):
            arrived(block * 2 + 1 - core, example, part)
            own_product(block * 2 + 1 - core, example, part)

    for part in range(HALVES):
        grad_copy(1, part).start()
    for part in range(HALVES):
        grad_copy(0, part).wait_recv()

    @pl.loop(0, PIECES)
    def _(piece):
        example, part = split(piece)
        slot = plane(2) * 2 + core
        arrived(slot, example, part)
        chunk_copy(slot, example, part, side_send.at[3 * PIECES + piece], sibling).start()
        slot = plane(-2) * 2 + core
        arrived(slot, example, part)
        chunk_copy(slot, example, part, far_send.at[2 * PIECES + piece], far).start()
        chunk_copy(slot, example, part, side_send.at[4 * PIECES + piece], sibling).start()
        for block in (plane(2), plane(-2)):
            own_product(block * 2 + core, example, part)
        for block in (plane(2), plane(-2)):
            arrived(block * 2 + 1 - core, example, part)
            own_product(block * 2 + 1 - core, example, part)

        @pl.when(piece < HALVES)
        def _():
            for parity in range(2):
                far_product(plane(2) * 2 + parity, 0, part)

    @pl.loop(0, PIECES)
    def _(piece):
        example, part = split(piece)
        slot = plane(3) * 2 + core
        arrived(slot, example, part)
        chunk_copy(slot, example, part, side_send.at[5 * PIECES + piece], sibling).start()
        own_product(slot, example, part)
        slot = plane(3) * 2 + 1 - core
        arrived(slot, example, part)
        own_product(slot, example, part)

        @pl.when(piece < HALVES)
        def _():
            for parity in range(2):
                far_product(plane(3) * 2 + parity, 0, part)

    for part in range(HALVES):
        grad_copy(1, part).wait_recv()

    @pl.loop(0, 2 * PIECES)
    def _(item):
        block = plane(2 + lax.div(item, PIECES))
        rest = lax.rem(item, PIECES)
        far_product(block * 2 + lax.div(rest, HALVES), 1, lax.rem(rest, HALVES))

    lanes = lax.broadcasted_iota(jnp.int32, (8, LANES), 1)

    def in_lanes(values):
        return jnp.where(lanes == 2 * data, values[0], jnp.where(lanes == 2 * data + 1, values[1], 0.0))

    own = [jnp.sum(jnp.sum(squares[example], axis=0, keepdims=True), axis=1, keepdims=True) for example in range(2)]
    square_box[tensor] = in_lanes(own)

    def square_copy(step, index):
        return pltpu.make_async_remote_copy(
            src_ref=square_box.at[tensor], dst_ref=square_box.at[tensor], send_sem=square_send.at[step],
            recv_sem=square_recv.at[index], device_id=(data, lax.rem(tensor + step, GROUP)), device_id_type=MESH)

    for step in FAR_TENSOR:
        square_copy(step, tensor).start()

    @pl.loop(0, SIDE_SENDS)
    def _(index):
        chunk_copy(0, 0, 0, side_send.at[index], sibling).wait_send()

        @pl.when(index < 3 * PIECES)
        def _():
            chunk_copy(0, 0, 0, far_send.at[index], far).wait_send()

        @pl.when(index < 2 * PIECES)
        def _():
            chunk_copy(0, 0, 0, near_send.at[index], near).wait_send()

    for example in range(2):
        for part in range(HALVES):
            grad_copy(example, part).wait_send()
    for step in reversed(FAR_TENSOR):
        square_copy(step, lax.rem(tensor + step, GROUP)).wait_recv()

    norm = jnp.sqrt(jnp.sum(square_box[...], axis=0) + 1e-6)
    norm_box[data] = in_lanes((norm, norm))

    def norm_copy(step, index):
        peer = lax.rem(place[0] + step // SIDE, SIDE) * SIDE + lax.rem(place[1] + step % SIDE, SIDE)
        return pltpu.make_async_remote_copy(
            src_ref=norm_box.at[data], dst_ref=norm_box.at[data], send_sem=norm_send.at[step],
            recv_sem=norm_recv.at[peer if index is None else index], device_id=(peer, tensor), device_id_type=MESH)

    for step in FAR_DATA:
        norm_copy(step, data).start()
    for step in range(1, GROUP):
        square_copy(step, tensor).wait_send()
    for step in reversed(FAR_DATA):
        norm_copy(step, None).wait_recv()

    norms = jnp.sum(norm_box[...], axis=0)[0:1]
    user_norm = jnp.sum(same_user[...] * norms, axis=2, keepdims=True)
    count = user_count[...]
    weight[...] = jnp.minimum(1.0, clip_bound * count / user_norm) / (count * counts.shape[0])

    def all_early(dim):
        whole = early[dim].at[pl.ds(0, SIDE - 1)]
        return pltpu.make_async_remote_copy(
            src_ref=whole, dst_ref=whole, send_sem=early_send.at[dim], recv_sem=early_recv.at[dim],
            device_id=sibling, device_id_type=MESH)

    def spot(dim, turn):
        if dim == 0:
            other = lax.rem(place[0] - missing + turn + SIDE, SIDE)
            return other, swap(place[0], other), other
        main = lax.rem(missing + turn, SIDE)
        return main, main, place[1]

    def target(dim, turn):
        _, main, other = spot(dim, turn)
        foreign = jnp.where(main == missing, 1, 0)
        row = lax.rem(main * SIDE + other - 4 * away * foreign + GROUP, GROUP)
        return row, plane(-foreign) * 2 + core

    def late_copy(dim, turn):
        return pltpu.make_async_remote_copy(
            src_ref=late.at[dim, turn], dst_ref=final.at[dim, place[1 - dim]], send_sem=total_send.at[dim, turn],
            recv_sem=total_recv.at[dim, place[1 - dim]], device_id=target(dim, turn), device_id_type=MESH)

    def is_here(dim, turn):
        row, column = target(dim, turn)
        return (row == data) & (column == tensor)

    for dim in range(2):
        all_early(dim).wait_recv()
    for turn in range(SIDE):
        for dim in range(2):
            index, main, other = spot(dim, turn)
            for part in range(HALVES):
                total = sum(decode(coded.at[main * SIDE + other, example, part, dim], weight[2 * data + example])
                            for example in range(2))
                for step in range(1, SIDE):
                    source = along(dim, step)
                    for example in range(2):
                        total = total + decode(early[dim].at[source, example, index, part],
                                               weight[2 * at(dim, source) + example])
                steps, powers = encode(total)
                late[dim, turn, part, 0:units] = steps
                late[dim, turn, part, units] = powers

            @pl.when(jnp.logical_not(is_here(dim, turn)))
            def _():
                late_copy(dim, turn).start()

            @pl.when(is_here(dim, turn))
            def _():
                pltpu.make_async_copy(
                    late.at[dim, turn], final.at[dim, place[1 - dim]], total_recv.at[dim, place[1 - dim]]).start()

    for dim in range(2):
        all_early(dim).wait_send()
    for step in range(1, GROUP):
        norm_copy(step, data).wait_send()
    for turn in range(SIDE):
        for dim in range(2):
            @pl.when(jnp.logical_not(is_here(dim, turn)))
            def _():
                late_copy(dim, turn).wait_send()

    for dim in range(2):
        for source in range(SIDE):
            pltpu.make_async_remote_copy(
                src_ref=late.at[0, 0], dst_ref=final.at[dim, source], send_sem=total_send.at[0, 0],
                recv_sem=total_recv.at[dim, source], device_id=sibling, device_id_type=MESH).wait_recv()
        for part in range(HALVES):
            total = sum(decode(final.at[dim, source, part], 1.0) for source in range(SIDE))
            out[pl.ds(2 * units * dim, 2 * units), :, pl.ds(part * LANES, LANES)] = total


def per_device(context, grad, users, counts):
    examples, length, width_in = context.shape
    width_out = grad.shape[2]
    tiles = width_out // 8
    units = width_out // 32
    dma = pltpu.SemaphoreType.DMA
    vmem = pltpu.VMEM
    int16 = jnp.int16
    clip_bound = 1.5 * math.sqrt(width_in * width_out * GROUP * GROUP)
    flops = 2 * examples * length * width_in * width_out * GROUP
    result = pl.pallas_call(
        functools.partial(kernel, clip_bound),
        out_shape=vmem((tiles, 8, width_in), F32),
        in_specs=[
            pl.BlockSpec(memory_space=pl.ANY),
            pl.BlockSpec(memory_space=pl.ANY),
            pl.BlockSpec(memory_space=pltpu.SMEM),
            pl.BlockSpec(memory_space=pltpu.SMEM),
        ],
        out_specs=pl.BlockSpec(memory_space=pltpu.VMEM),
        scratch_shapes=[
            vmem((GROUP, examples, HALVES, length, LANES), context.dtype),
            vmem((examples, HALVES, 16 * units, length), grad.dtype),
            vmem((examples, HALVES, 16 * units, length), grad.dtype),
            vmem((GROUP, examples, HALVES, HALVES, units + 1, 16, LANES), int16),
            vmem((SIDE, examples, SIDE, HALVES, units + 1, 16, LANES), int16),
            vmem((SIDE, examples, SIDE, HALVES, units + 1, 16, LANES), int16),
            vmem((2, SIDE, HALVES, units + 1, 16, LANES), int16),
            vmem((2, SIDE, HALVES, units + 1, 16, LANES), int16),
            vmem((2 * GROUP, 1, LANES), F32),
            vmem((2 * GROUP, 1, LANES), F32),
            vmem((2 * GROUP, 1, LANES), F32),
            vmem((examples, 8, LANES), F32),
            vmem((GROUP, 8, LANES), F32),
            vmem((GROUP, 8, LANES), F32),
            dma((2 * PIECES,)),
            dma((GROUP, 2, HALVES)),
            dma((3 * PIECES,)),
            dma((2 * PIECES,)),
            dma((SIDE_SENDS,)),
            dma((2, HALVES)),
            dma((2, HALVES)),
            dma((2,)),
            dma((2,)),
            dma((GROUP,)),
            dma((GROUP,)),
            dma((GROUP,)),
            dma((GROUP,)),
            dma((2, SIDE)),
            dma((2, SIDE)),
            pltpu.SemaphoreType.REGULAR((3,)),
        ],
        compiler_params=pltpu.CompilerParams(
            collective_id=0, has_side_effects=True, vmem_limit_bytes=56 * 2**20),
        cost_estimate=pl.CostEstimate(flops=flops, bytes_accessed=2 * context.size + 2 * grad.size, transcendentals=0),
    )(context, jnp.swapaxes(grad, 1, 2), users, counts)
    return result.reshape(width_out, width_in).T


def solution(mesh):
    in_specs = (P("dp", None, "tensor"), P("dp", None, "tensor"), P(), P())
    out_specs = P("dp", "tensor")
    return jax.shard_map(
        per_device, mesh=mesh, in_specs=in_specs, out_specs=out_specs, check_vma=False
    )
```

time: 110 us -> 106 us (0.964)
  Pallas kernels: 109 us -> 105 us
    pallas_call x1, Pallas kernels: 109 us -> 105 us  [per_device(): pl.pallas_call(functools.partial(kernel, clip_bound), out_shape=vmem((til...]
where the time goes in v5:
time: 106 us
  Pallas kernels  105 us (99%)
    pallas_call x1, Pallas kernels, per_device(): pl.pallas_call(functools.partial(kernel, clip_bound), out_shape=vmem((til...  105 us

profile of v5, /device:TPU:1, one launch (start us, length us, event | category | flops | bytes accessed | tf_op | source)
XLA Modules:
  0.0 105.6 jit_solution(5028875328268239873)
XLA Ops:
  0.0 104.9 %shard_map.46 = f32[36,8,256]{2,1,0:T(8,128)S(1)} custom-call(bf16[2,1024,256]{2,1,0:T(8,128)(2,1)} %context.1, bf16[2,288,1024]{2,1,0:T(8,128)(2,1)} %bitcast.5, s32[32]{0:T(128)} %users.1, s32[16]{0:T(128)} %counts.1), custom_call_target="tpu_custom_call" | custom-call | flops 4831838208 | bytes 2228224 | tf_op jit(solution)/shard_map/pallas_call | solution.py:377
  104.9 0.7 copy.6

commit v6 on v5

--- a/solution.py
+++ b/solution.py
@@ -38,7 +38,7 @@
     return scale * steps.reshape((2 * units, 8) + ref.shape[2:])
 
 
-def kernel(clip_bound, context, grad, users, counts, out, held, grad_own, grad_far, coded, early_x, early_y, late, final,
+def kernel(clip_bound, context, grad, users, counts, out, held, grad_own, grad_far, coded, early_x, early_y, late, final, spare,
            same_user, user_count, weight, squares, square_box, norm_box,
            local_sem, ring_recv, far_send, near_send, side_send, grad_send, grad_recv, early_send, early_recv,
            square_send, square_recv, norm_send, norm_recv, total_send, total_recv, hello):
@@ -128,11 +128,7 @@
         moved = lax.rem(missing + other, SIDE)
         return jnp.where(main == missing, moved, jnp.where(main == moved, missing, main))
 
-    def product(lhs, slot, example, part, tile):
-        lhs = lhs.reshape((2 * rows, lhs.shape[2]))
-        term = jnp.dot(lhs, held[slot, example, part], preferred_element_type=F32)
-        tiles = term.reshape((4 * units, 8, LANES))
-        squares[example] += jnp.sum(tiles * tiles, axis=0)
+    def ship(tiles, tile, example, part):
         main, other = lax.div(tile, SIDE), lax.rem(tile, SIDE)
         for half in range(2):
             steps, powers = encode(tiles[2 * units * half:2 * units * (half + 1)])
@@ -147,6 +143,13 @@
                     dst_ref=early[half].at[place[half], example, (other, main)[half], part],
                     send_sem=early_send.at[half], recv_sem=early_recv.at[half],
                     device_id=(at(half, owner), tensor), device_id_type=MESH).start()
+
+    def product(lhs, slot, example, part, tile):
+        lhs = lhs.reshape((2 * rows, lhs.shape[2]))
+        term = jnp.dot(lhs, held[slot, example, part], preferred_element_type=F32)
+        tiles = term.reshape((4 * units, 8, LANES))
+        squares[example] += jnp.sum(tiles * tiles, axis=0)
+        ship(tiles, tile, example, part)
 
     def own_product(slot, example, part):
         product(grad_own[example], slot, example, part, slot)
@@ -229,11 +232,18 @@
     for part in range(HALVES):
         grad_copy(1, part).wait_recv()
 
-    @pl.loop(0, 2 * PIECES)
+    @pl.loop(0, 4)
     def _(item):
-        block = plane(2 + lax.div(item, PIECES))
-        rest = lax.rem(item, PIECES)
-        far_product(block * 2 + lax.div(rest, HALVES), 1, lax.rem(rest, HALVES))
+        slot = plane(2 + lax.div(item, 2)) * 2 + lax.rem(item, 2)
+        lhs = grad_far[1]
+        rhs = jnp.concatenate([held[slot, 1, part] for part in range(HALVES)], axis=1)
+        term = jnp.dot(lhs.reshape((2 * rows, lhs.shape[2])), rhs, preferred_element_type=F32)
+        tiles = term.reshape((4 * units, 8, HALVES * LANES))
+        square = jnp.sum(tiles * tiles, axis=0)
+        for part in range(HALVES):
+            span = slice(part * LANES, (part + 1) * LANES)
+            squares[1] += square[:, span]
+            spare[item, part] = tiles[:, :, span]
 
     lanes = lax.broadcasted_iota(jnp.int32, (8, LANES), 1)
 
@@ -250,6 +260,12 @@
 
     for step in FAR_TENSOR:
         square_copy(step, tensor).start()
+
+    @pl.loop(0, 4)
+    def _(item):
+        tile = lax.rem((plane(2 + lax.div(item, 2)) + 2 * away) * 2 + lax.rem(item, 2) + 2 * RING, 2 * RING)
+        for part in range(HALVES):
+            ship(spare[item, part], tile, 1, part)
 
     @pl.loop(0, SIDE_SENDS)
     def _(index):
@@ -297,10 +313,13 @@
             device_id=sibling, device_id_type=MESH)
 
     def spot(dim, turn):
+        first = lax.rem((place[0] - missing if dim == 0 else missing) - place[1 - dim] * (1 - dim) - place[0] * dim + 2 * SIDE, SIDE)
+        step = (first, jnp.where(first == 2, 1, 2), jnp.where((first == 1) | (first == 2), 3, 1),
+                jnp.where(first == 0, 3, 0))[turn]
         if dim == 0:
-            other = lax.rem(place[0] - missing + turn + SIDE, SIDE)
+            other = lax.rem(place[1] + step, SIDE)
             return other, swap(place[0], other), other
-        main = lax.rem(missing + turn, SIDE)
+        main = lax.rem(place[0] + step, SIDE)
         return main, main, place[1]
 
     def target(dim, turn):
@@ -393,6 +412,7 @@
             vmem((SIDE, examples, SIDE, HALVES, units + 1, 16, LANES), int16),
             vmem((2, SIDE, HALVES, units + 1, 16, LANES), int16),
             vmem((2, SIDE, HALVES, units + 1, 16, LANES), int16),
+            vmem((4, HALVES, tiles, 8, LANES), F32),
             vmem((2 * GROUP, 1, LANES), F32),
             vmem((2 * GROUP, 1, LANES), F32),
             vmem((2 * GROUP, 1, LANES), F32),

time: 106 us -> 104 us (0.981)
  Pallas kernels: 105 us -> 103 us
    pallas_call x1, Pallas kernels: 105 us -> 103 us  [per_device(): pl.pallas_call(functools.partial(kernel, clip_bound), out_shape=vmem((til...]
where the time goes in v6:
time: 104 us
  Pallas kernels  103 us (99%)
    pallas_call x1, Pallas kernels, per_device(): pl.pallas_call(functools.partial(kernel, clip_bound), out_shape=vmem((til...  103 us

profile of v6, /device:TPU:1, one launch (start us, length us, event | category | flops | bytes accessed | tf_op | source)
XLA Modules:
  0.0 103.7 jit_solution(17550115074552507612)
XLA Ops:
  0.0 102.9 %shard_map.46 = f32[36,8,256]{2,1,0:T(8,128)S(1)} custom-call(bf16[2,1024,256]{2,1,0:T(8,128)(2,1)} %context.1, bf16[2,288,1024]{2,1,0:T(8,128)(2,1)} %bitcast.5, s32[32]{0:T(128)} %users.1, s32[16]{0:T(128)} %counts.1), custom_call_target="tpu_custom_call" | custom-call | flops 4831838208 | bytes 2228224 | tf_op jit(solution)/shard_map/pallas_call | solution.py:396
  102.9 0.7 copy.6

commit v7 on v6

--- a/solution.py
+++ b/solution.py
@@ -79,8 +79,6 @@
                 local_sem.at[PIECES + number]))
     for copy in loads:
         copy.start()
-    for copy in loads:
-        copy.wait()
 
     pl.semaphore_wait(barrier, 7)
 
@@ -89,22 +87,27 @@
             src_ref=held.at[slot, example, part], dst_ref=held.at[slot, example, part], send_sem=send_sem,
             recv_sem=ring_recv.at[slot, example, part], device_id=device, device_id_type=MESH)
 
+    def own_copy(example, part, send_sem, device):
+        return pltpu.make_async_remote_copy(
+            src_ref=context.at[example, :, pl.ds(part * LANES, LANES)], dst_ref=held.at[tensor, example, part],
+            send_sem=send_sem, recv_sem=ring_recv.at[tensor, example, part], device_id=device, device_id_type=MESH)
+
     def grad_copy(example, part):
         return pltpu.make_async_remote_copy(
-            src_ref=grad_own.at[example, part], dst_ref=grad_far.at[example, part],
+            src_ref=grad.at[example, pl.ds(part * rows, rows)], dst_ref=grad_far.at[example, part],
             send_sem=grad_send.at[example, part], recv_sem=grad_recv.at[example, part],
             device_id=near, device_id_type=MESH)
 
     for part in range(HALVES):
         grad_copy(0, part).start()
-        chunk_copy(tensor, 0, part, far_send.at[part], far).start()
+        own_copy(0, part, far_send.at[part], far).start()
     for piece in range(PIECES):
         example, part = piece // HALVES, piece % HALVES
-        chunk_copy(tensor, example, part, near_send.at[piece], near).start()
+        own_copy(example, part, near_send.at[piece], near).start()
         if example == 1:
-            chunk_copy(tensor, example, part, far_send.at[piece], far).start()
+            own_copy(example, part, far_send.at[piece], far).start()
     for piece in range(PIECES):
-        chunk_copy(tensor, piece // HALVES, piece % HALVES, side_send.at[piece], sibling).start()
+        own_copy(piece // HALVES, piece % HALVES, side_send.at[piece], sibling).start()
 
     for turn in range(3):
         for device in around:
@@ -162,6 +165,9 @@
 
     def split(piece):
         return lax.div(piece, HALVES), lax.rem(piece, HALVES)
+
+    for copy in loads:
+        copy.wait()
 
     @pl.loop(0, PIECES)
     def _(piece):
@@ -314,8 +320,10 @@
 
     def spot(dim, turn):
         first = lax.rem((place[0] - missing if dim == 0 else missing) - place[1 - dim] * (1 - dim) - place[0] * dim + 2 * SIDE, SIDE)
-        step = (first, jnp.where(first == 2, 1, 2), jnp.where((first == 1) | (first == 2), 3, 1),
-                jnp.where(first == 0, 3, 0))[turn]
+        order = (first, jnp.where(first == 2, 1, 2), jnp.where((first == 1) | (first == 2), 3, 1),
+                 jnp.where(first == 0, 3, 0))
+        swapped = (order[0], order[2], order[1], order[3])
+        step = jnp.where(core == dim, order[turn], swapped[turn])
         if dim == 0:
             other = lax.rem(place[1] + step, SIDE)
             return other, swap(place[0], other), other

time: 104 us -> 103 us (level)
  no operation moved by 1% of the time
where the time goes in v7:
time: 103 us
  Pallas kernels  102 us (99%)
    pallas_call x1, Pallas kernels, per_device(): pl.pallas_call(functools.partial(kernel, clip_bound), out_shape=vmem((til...  102 us

profile of v7, /device:TPU:1, one launch (start us, length us, event | category | flops | bytes accessed | tf_op | source)
XLA Modules:
  0.0 103.0 jit_solution(8093771493926862000)
XLA Ops:
  0.0 102.3 %shard_map.46 = f32[36,8,256]{2,1,0:T(8,128)S(1)} custom-call(bf16[2,1024,256]{2,1,0:T(8,128)(2,1)} %context.1, bf16[2,288,1024]{2,1,0:T(8,128)(2,1)} %bitcast.5, s32[32]{0:T(128)} %users.1, s32[16]{0:T(128)} %counts.1), custom_call_target="tpu_custom_call" | custom-call | flops 4831838208 | bytes 2228224 | tf_op jit(solution)/shard_map/pallas_call | solution.py:404
  102.3 0.7 copy.6

commit v8 on v7

--- a/solution.py
+++ b/solution.py
@@ -36,6 +36,13 @@
     scale = factor * (jnp.exp2(power) * (1.0 / STEPS))
     steps = ref[0:units].astype(jnp.int32).astype(F32)
     return scale * steps.reshape((2 * units, 8) + ref.shape[2:])
+
+
+def landed(ref, part):
+    units = ref.shape[0] // 2
+    power = ref[2 * units].astype(jnp.int32).astype(F32)[8 * part:8 * part + 1]
+    steps = ref[part * units:(part + 1) * units].astype(jnp.int32).astype(F32)
+    return (jnp.exp2(power) * (1.0 / STEPS)) * steps.reshape((2 * units, 8) + ref.shape[2:])
 
 
 def kernel(clip_bound, context, grad, users, counts, out, held, grad_own, grad_far, coded, early_x, early_y, late, final, spare,
@@ -350,6 +357,7 @@
     for turn in range(SIDE):
         for dim in range(2):
             index, main, other = spot(dim, turn)
+            both = []
             for part in range(HALVES):
                 total = sum(decode(coded.at[main * SIDE + other, example, part, dim], weight[2 * data + example])
                             for example in range(2))
@@ -359,8 +367,10 @@
                         total = total + decode(early[dim].at[source, example, index, part],
                                                weight[2 * at(dim, source) + example])
                 steps, powers = encode(total)
-                late[dim, turn, part, 0:units] = steps
-                late[dim, turn, part, units] = powers
+                late[dim, turn, part * units:(part + 1) * units] = steps
+                both.append(powers.astype(jnp.int32))
+            upper = lax.broadcasted_iota(jnp.int32, both[0].shape, 0) < 8
+            late[dim, turn, 2 * units] = jnp.where(upper, both[0], both[1]).astype(jnp.int16)
 
             @pl.when(jnp.logical_not(is_here(dim, turn)))
             def _():
@@ -387,7 +397,7 @@
                 src_ref=late.at[0, 0], dst_ref=final.at[dim, source], send_sem=total_send.at[0, 0],
                 recv_sem=total_recv.at[dim, source], device_id=sibling, device_id_type=MESH).wait_recv()
         for part in range(HALVES):
-            total = sum(decode(final.at[dim, source, part], 1.0) for source in range(SIDE))
+            total = sum(landed(final.at[dim, source], part) for source in range(SIDE))
             out[pl.ds(2 * units * dim, 2 * units), :, pl.ds(part * LANES, LANES)] = total
 
 
@@ -418,8 +428,8 @@
             vmem((GROUP, examples, HALVES, HALVES, units + 1, 16, LANES), int16),
             vmem((SIDE, examples, SIDE, HALVES, units + 1, 16, LANES), int16),
             vmem((SIDE, examples, SIDE, HALVES, units + 1, 16, LANES), int16),
-            vmem((2, SIDE, HALVES, units + 1, 16, LANES), int16),
-            vmem((2, SIDE, HALVES, units + 1, 16, LANES), int16),
+            vmem((2, SIDE, 2 * units + 1, 16, LANES), int16),
+            vmem((2, SIDE, 2 * units + 1, 16, LANES), int16),
             vmem((4, HALVES, tiles, 8, LANES), F32),
             vmem((2 * GROUP, 1, LANES), F32),
             vmem((2 * GROUP, 1, LANES), F32),

time: 103 us -> 103 us (level)
  no operation moved by 1% of the time
where the time goes in v8:
time: 103 us
  Pallas kernels  102 us (99%)
    pallas_call x1, Pallas kernels, per_device(): pl.pallas_call(functools.partial(kernel, clip_bound), out_shape=vmem((til...  102 us

profile of v8, /device:TPU:1, one launch (start us, length us, event | category | flops | bytes accessed | tf_op | source)
XLA Modules:
  0.0 102.8 jit_solution(9442757859446622782)
XLA Ops:
  0.0 102.1 %shard_map.46 = f32[36,8,256]{2,1,0:T(8,128)S(1)} custom-call(bf16[2,1024,256]{2,1,0:T(8,128)(2,1)} %context.1, bf16[2,288,1024]{2,1,0:T(8,128)(2,1)} %bitcast.5, s32[32]{0:T(128)} %users.1, s32[16]{0:T(128)} %counts.1), custom_call_target="tpu_custom_call" | custom-call | flops 4831838208 | bytes 2228224 | tf_op jit(solution)/shard_map/pallas_call | solution.py:414
  102.1 0.7 copy.6

commit v9 on v7

--- a/solution.py
+++ b/solution.py
@@ -238,9 +238,8 @@
     for part in range(HALVES):
         grad_copy(1, part).wait_recv()
 
-    @pl.loop(0, 4)
-    def _(item):
-        slot = plane(2 + lax.div(item, 2)) * 2 + lax.rem(item, 2)
+    for item in range(4):
+        slot = plane(2 + item // 2) * 2 + item % 2
         lhs = grad_far[1]
         rhs = jnp.concatenate([held[slot, 1, part] for part in range(HALVES)], axis=1)
         term = jnp.dot(lhs.reshape((2 * rows, lhs.shape[2])), rhs, preferred_element_type=F32)

time: 103 us -> 103 us (level)
  no operation moved by 1% of the time
where the time goes in v9:
time: 103 us; the launch traced here: 102 us
  Pallas kernels  102 us (99%)
    pallas_call x1, Pallas kernels, per_device(): pl.pallas_call(functools.partial(kernel, clip_bound), out_shape=vmem((til...  102 us

profile of v9, /device:TPU:1, one launch (start us, length us, event | category | flops | bytes accessed | tf_op | source)
XLA Modules:
  0.0 102.4 jit_solution(7414269456093100157)
XLA Ops:
  0.0 101.7 %shard_map.46 = f32[36,8,256]{2,1,0:T(8,128)S(1)} custom-call(bf16[2,1024,256]{2,1,0:T(8,128)(2,1)} %context.1, bf16[2,288,1024]{2,1,0:T(8,128)(2,1)} %bitcast.5, s32[32]{0:T(128)} %users.1, s32[16]{0:T(128)} %counts.1), custom_call_target="tpu_custom_call" | custom-call | flops 4831838208 | bytes 2228224 | tf_op jit(solution)/shard_map/pallas_call | solution.py:403
  101.7 0.7 copy.6
